TPU v7x, 256 devices: a whole 4x4x8 slice. The times are simulated.
256 devices in a mesh: base: 32 (over x, y, core), band: 8 (over z).
Axes of the slice: x: 4, y: 4, z: 8, core: 2. Of those that a mesh axis runs over, the one named last changes fastest.
Arguments:
- visibilities: float32 [65536, 2, 128], P(('base', 'band')), may hold values from -6 to 6
- coords: float32 [65536, 2, 8], P(('base', 'band')), may hold values from -11.2 to 11.2
- chan_scale: float32 [16], replicated, may hold values from 0.9 to 1.1
- taper_gain: float32 [32, 32], replicated, may hold values from 0.25 to 1
- owner_base: int32 [65536, 1], P(('base', 'band')), may hold values from 0 to 31; in each aligned block of 256 rows (0 to 255, 256 to 511, ...) at most 16 rows name the same one
- tile_cell: int32 [65536], P(('base', 'band')), may hold values from 0 to 255
Outputs:
- image: float32 [2, 8192, 8192], P(None, ('base', 'band'))
Inputs may be any that keep to these rules, and one draw needn't show every extreme that they name: `owner_base`: among the 256 baselines of one device no value occurs more than 16 times, and in every draw some device has a value exactly 16 times.
All inputs are finite; a program needn't handle non-finite values.
Results may differ from a plain program's by a relative error of at most 0.0003.
Values sent between devices are 32-bit elements; how exact they have to be, the bound alone decides.
A program may use at most 128 MiB of HBM per device.

v0:
```python
import math

import jax
import jax.numpy as jnp
from jax import lax
from jax.sharding import PartitionSpec as P

G = 8192


two_pi = 2.0 * math.pi
exact = lax.Precision.HIGHEST


def phase_table(length, direction):
    indices = jnp.arange(length, dtype=jnp.int32)
    product = indices[:, None] * indices[None, :] % length
    angle = direction * two_pi / length * product.astype(jnp.float32)
    return (jnp.cos(angle), jnp.sin(angle))


def grid_block(samples, places, chan_scale, taper_gain):
    number = samples.shape[0]
    extent = taper_gain.shape[0]
    time_count = places.shape[2]
    sample_count = time_count * chan_scale.shape[0]
    offsets = (jnp.arange(extent, dtype=jnp.float32) - extent // 2) / extent
    u_pos = (places[:, 0, :, None] * chan_scale[None, None, :]).reshape(number, sample_count)
    v_pos = (places[:, 1, :, None] * chan_scale[None, None, :]).reshape(number, sample_count)
    angle_y = two_pi * offsets[None, :, None] * v_pos[:, None, :]
    angle_x = two_pi * offsets[None, :, None] * u_pos[:, None, :]
    cos_y = jnp.cos(angle_y)
    sin_y = jnp.sin(angle_y)
    cos_x = jnp.cos(angle_x)
    sin_x = jnp.sin(angle_x)
    real_in = samples[:, 0:1, :]
    imag_in = samples[:, 1:2, :]
    left_re = real_in * cos_y - imag_in * sin_y
    left_im = real_in * sin_y + imag_in * cos_y

    def pairwise(first_arr, second_arr):
        return jnp.einsum("nyv,nxv->nyx", first_arr, second_arr, precision=exact)

    pix_re = (pairwise(left_re, cos_x) - pairwise(left_im, sin_x)) * taper_gain
    pix_im = (pairwise(left_re, sin_x) + pairwise(left_im, cos_x)) * taper_gain
    f_cos, f_sin = phase_table(extent, 1.0)

    def along_x(values, table):
        return jnp.einsum("nyx,xk->nyk", values, table, precision=exact)

    def along_y(values, table):
        return jnp.einsum("yk,nyx->nkx", table, values, precision=exact)

    q_re = along_x(pix_re, f_cos) + along_x(pix_im, f_sin)
    q_im = along_x(pix_im, f_cos) - along_x(pix_re, f_sin)
    t_re = along_y(q_re, f_cos) + along_y(q_im, f_sin)
    t_im = along_y(q_im, f_cos) - along_y(q_re, f_sin)
    factor = 1.0 / (extent * math.sqrt(sample_count))
    return jnp.stack([t_re, t_im], axis=1).reshape(number, 2, extent * extent) * factor


def make_tiles(samples, places, chan_scale, taper_gain):
    number = samples.shape[0]
    block_size = math.gcd(number, 64)
    blocks = number // block_size

    def one_block(pieces):
        return grid_block(pieces[0], pieces[1], chan_scale, taper_gain)

    result = lax.map(
        one_block,
        (
            samples.reshape(blocks, block_size, 2, samples.shape[2]),
            places.reshape(blocks, block_size, 2, places.shape[2]),
        ),
    )
    return result.reshape(number, 2, result.shape[3])


def dft_last(real_part, imag_part):
    row_count = real_part.shape[0]
    length = real_part.shape[1]
    first_len = 2 ** ((length.bit_length() - 1) // 2)
    second_len = length // first_len
    cos_one, sin_one = phase_table(first_len, 1.0)
    cos_two, sin_two = phase_table(second_len, 1.0)
    real_in = real_part.reshape(row_count, first_len, second_len)
    imag_in = imag_part.reshape(row_count, first_len, second_len)

    def mix_first(values, table):
        return jnp.einsum("pab,ak->pkb", values, table, precision=exact)

    y_re = mix_first(real_in, cos_one) - mix_first(imag_in, sin_one)
    y_im = mix_first(real_in, sin_one) + mix_first(imag_in, cos_one)
    first_ids = jnp.arange(first_len, dtype=jnp.int32)
    second_ids = jnp.arange(second_len, dtype=jnp.int32)
    turns = first_ids[:, None] * second_ids[None, :] % length
    twist = two_pi / length * turns.astype(jnp.float32)
    twist_cos = jnp.cos(twist)
    twist_sin = jnp.sin(twist)
    z_re = y_re * twist_cos - y_im * twist_sin
    z_im = y_re * twist_sin + y_im * twist_cos

    def mix_second(values, table):
        return jnp.einsum("pkb,bm->pmk", values, table, precision=exact)

    out_re = mix_second(z_re, cos_two) - mix_second(z_im, sin_two)
    out_im = mix_second(z_re, sin_two) + mix_second(z_im, cos_two)
    return (out_re.reshape(row_count, length), out_im.reshape(row_count, length))


def shards(visibilities, coords, chan_scale, taper_gain, owner_base, tile_cell):
    n_base = lax.axis_size("base")
    n_band = lax.axis_size("band")
    slot_count = visibilities.shape[0]
    extent = taper_gain.shape[0]
    area = extent * extent
    capacity = 2 * slot_count // n_base
    buffer_len = capacity * n_base
    owners = owner_base[:, 0]
    onehot = (owners[:, None] == jnp.arange(n_base, dtype=jnp.int32)[None, :]).astype(jnp.int32)
    before = jnp.cumsum(onehot, axis=0) - onehot
    rank_in = jnp.sum(before * onehot, axis=1)
    target = rank_in * n_base + owners
    cell_slots = jnp.zeros((buffer_len,), jnp.float32).at[target].set(tile_cell.astype(jnp.float32))
    cell_slots = cell_slots.reshape(capacity, n_base)
    tiles = make_tiles(visibilities, coords, chan_scale, taper_gain)
    packed = jnp.zeros((buffer_len, 2, area), jnp.float32).at[target].set(tiles)
    packed = packed.reshape(capacity, n_base, 2, area)
    arrived, arrived_cells = (
        lax.all_to_all(packed, "base", split_axis=1, concat_axis=1, tiled=True),
        lax.all_to_all(cell_slots, "base", split_axis=1, concat_axis=1, tiled=True),
    )
    row_tiles = G // (extent * n_band)
    col_tiles = G // (extent * n_base)
    segment_ids = arrived_cells.reshape(buffer_len).astype(jnp.int32)
    summed = jax.ops.segment_sum(
        arrived.reshape(buffer_len, 2 * area), segment_ids, num_segments=row_tiles * col_tiles
    )
    uv_grid = summed.reshape(row_tiles, col_tiles, 2, extent, extent).transpose(2, 0, 3, 1, 4)
    uv_grid = uv_grid.reshape(2, row_tiles * extent, col_tiles * extent)
    row_major = lax.all_to_all(uv_grid, "base", split_axis=1, concat_axis=2, tiled=True)
    row_re, row_im = dft_last(row_major[0], row_major[1])
    returned = lax.all_to_all(
        jnp.stack([row_re, row_im]), "base", split_axis=2, concat_axis=1, tiled=True
    )
    flipped = jnp.transpose(returned, (0, 2, 1))
    col_major = lax.all_to_all(flipped, "band", split_axis=1, concat_axis=2, tiled=True)
    col_re, col_im = dft_last(col_major[0], col_major[1])
    return jnp.stack([col_re, col_im]) * (1.0 / G)


def solution(mesh):
    placed = (
        P(("base", "band"), None, None),
        P(("base", "band"), None, None),
        P(),
        P(),
        P(("base", "band"), None),
        P(("base", "band")),
    )
    return jax.shard_map(
        shards,
        mesh=mesh,
        in_specs=placed,
        out_specs=P(None, ("base", "band"), None),
        check_vma=False,
    )
```

profile of v0, /device:TPU:1, one launch (start us, length us, event | category | flops | bytes accessed | tf_op | source)
XLA Modules:
  0.0 582.0 jit_solution(8600578806524166067)
XLA Ops:
  5.8 8.6 %all-to-all-start = ((f32[16,32,1]{0,2,1:T(1,128)}), f32[16,32,1]{0,2,1:T(1,128)S(1)}, u32[]{:S(2)}, u32[]{:S(2)}) async-start(f32[16,32,1]{0,2,1:T(1,128)} %copy.184), calls=%async_computation | async-start | bytes 32768 | tf_op jit(solution)/shard_map/all_to_all | solution.py:132
  15.2 196.9 %while.12 = (s32[]{:T(128)}, f32[4,64,2,1024]{3,1,0,2:T(8,128)}, f32[4,64,2,128]{3,2,1,0:T(2,128)}, f32[4,64,2,8]{1,0,3,2:T(4,128)S(1)}, f32[16]{0:T(128)}, /*index=5*/f32[32,32]{1,0:T(8,128)}, s32[]{:T(128)}) while((s32[]{:T(128)}, f32[4,64,2,1024]{3,1,0,2:T(8,128)}, f32[4,64,2,128]{3,2,1,0:T(2,128)}, f32[4,64,2,8]{1,0,3,2:T(4,128)S(1)}, ...), condition=%wide.region_5.6_spmd, body=%wide.region_4.5_spmd.sunk | while | flops 610140224 | bytes 13221169 | solution.py:70
  17.4 8.9 %fusion.319 = f32[64,32,32]{2,1,0:T(8,128)S(1)} fusion(f32[64,128]{1,0:T(8,128)S(1)} %copy.248, f32[64,128]{1,0:T(8,128)S(1)} %get-tuple-element.192, f32[64,128]{1,0:T(8,128)S(1)} %copy.250, f32[32]{0:T(128)S(1)} %add_multiply_fusion.2, f32[64,128]{1,0:T(8,128)S(1)} %get-tuple-element.194), kind=kOutput, calls=%fused_computation.12.clone.1 | convolution fusion | flops 101974016 | bytes 393344 | tf_op jit(solution)/shard_map/while/body/eval_jaxpr/nyv,nxv->nyx/dot_general | solution.py:42
  26.3 9.4 %fusion.320 = f32[64,32,32]{2,1,0:T(8,128)S(1)} fusion(f32[64,32,32]{2,1,0:T(8,128)S(1)} %fusion.319, f32[32,32]{1,0:T(8,128)S(1)} %copy-done.2, f32[64,128]{1,0:T(8,128)S(1)} %copy.248, f32[64,128]{1,0:T(8,128)S(1)} %get-tuple-element.192, f32[64,128]{1,0:T(8,128)S(1)} %copy.250, f32[32]{0:T(128)S(1)} %add_multiply_fusion.2, ...), kind=kOutput, calls=%fused_computation.18.clone.1 | convolution fusion | flops 102105088 | bytes 659584 | tf_op jit(solution)/shard_map/while/body/eval_jaxpr/nyv,nxv->nyx/dot_general | solution.py:42
  37.0 9.0 %fusion.316 = f32[64,32,32]{2,1,0:T(8,128)S(1)} fusion(f32[64,128]{1,0:T(8,128)S(1)} %copy.248, f32[64,128]{1,0:T(8,128)S(1)} %get-tuple-element.192, f32[64,128]{1,0:T(8,128)S(1)} %copy.250, f32[32]{0:T(128)S(1)} %add_multiply_fusion.2, f32[64,128]{1,0:T(8,128)S(1)} %get-tuple-element.194), kind=kOutput, calls=%fused_computation.11.clone.1 | convolution fusion | flops 101974016 | bytes 393344 | tf_op jit(solution)/shard_map/while/body/eval_jaxpr/nyv,nxv->nyx/dot_general | solution.py:42
  46.0 9.1 %fusion.317 = f32[64,32,32]{2,1,0:T(8,128)S(1)} fusion(f32[64,32,32]{2,1,0:T(8,128)S(1)} %fusion.316, f32[32,32]{1,0:T(8,128)S(1)} %copy-done.2, f32[64,128]{1,0:T(8,128)S(1)} %copy.248, f32[64,128]{1,0:T(8,128)S(1)} %get-tuple-element.192, f32[64,128]{1,0:T(8,128)S(1)} %copy.250, f32[32]{0:T(128)S(1)} %add_multiply_fusion.2, ...), kind=kOutput, calls=%fused_computation.17.clone.1 | convolution fusion | flops 102105088 | bytes 659584 | tf_op jit(solution)/shard_map/while/body/eval_jaxpr/nyv,nxv->nyx/dot_general | solution.py:42
  65.8 8.9 %fusion.319 = f32[64,32,32]{2,1,0:T(8,128)S(1)} fusion(f32[64,128]{1,0:T(8,128)S(1)} %copy.248, f32[64,128]{1,0:T(8,128)S(1)} %get-tuple-element.192, f32[64,128]{1,0:T(8,128)S(1)} %copy.250, f32[32]{0:T(128)S(1)} %add_multiply_fusion.2, f32[64,128]{1,0:T(8,128)S(1)} %get-tuple-element.194), kind=kOutput, calls=%fused_computation.12.clone.1 | convolution fusion | flops 101974016 | bytes 393344 | tf_op jit(solution)/shard_map/while/body/eval_jaxpr/nyv,nxv->nyx/dot_general | solution.py:42
  74.6 9.1 %fusion.320 = f32[64,32,32]{2,1,0:T(8,128)S(1)} fusion(f32[64,32,32]{2,1,0:T(8,128)S(1)} %fusion.319, f32[32,32]{1,0:T(8,128)S(1)} %copy-done.2, f32[64,128]{1,0:T(8,128)S(1)} %copy.248, f32[64,128]{1,0:T(8,128)S(1)} %get-tuple-element.192, f32[64,128]{1,0:T(8,128)S(1)} %copy.250, f32[32]{0:T(128)S(1)} %add_multiply_fusion.2, ...), kind=kOutput, calls=%fused_computation.18.clone.1 | convolution fusion | flops 102105088 | bytes 659584 | tf_op jit(solution)/shard_map/while/body/eval_jaxpr/nyv,nxv->nyx/dot_general | solution.py:42
  84.9 9.1 %fusion.316 = f32[64,32,32]{2,1,0:T(8,128)S(1)} fusion(f32[64,128]{1,0:T(8,128)S(1)} %copy.248, f32[64,128]{1,0:T(8,128)S(1)} %get-tuple-element.192, f32[64,128]{1,0:T(8,128)S(1)} %copy.250, f32[32]{0:T(128)S(1)} %add_multiply_fusion.2, f32[64,128]{1,0:T(8,128)S(1)} %get-tuple-element.194), kind=kOutput, calls=%fused_computation.11.clone.1 | convolution fusion | flops 101974016 | bytes 393344 | tf_op jit(solution)/shard_map/while/body/eval_jaxpr/nyv,nxv->nyx/dot_general | solution.py:42
  94.0 9.3 %fusion.317 = f32[64,32,32]{2,1,0:T(8,128)S(1)} fusion(f32[64,32,32]{2,1,0:T(8,128)S(1)} %fusion.316, f32[32,32]{1,0:T(8,128)S(1)} %copy-done.2, f32[64,128]{1,0:T(8,128)S(1)} %copy.248, f32[64,128]{1,0:T(8,128)S(1)} %get-tuple-element.192, f32[64,128]{1,0:T(8,128)S(1)} %copy.250, f32[32]{0:T(128)S(1)} %add_multiply_fusion.2, ...), kind=kOutput, calls=%fused_computation.17.clone.1 | convolution fusion | flops 102105088 | bytes 659584 | tf_op jit(solution)/shard_map/while/body/eval_jaxpr/nyv,nxv->nyx/dot_general | solution.py:42
  113.7 8.9 %fusion.319 = f32[64,32,32]{2,1,0:T(8,128)S(1)} fusion(f32[64,128]{1,0:T(8,128)S(1)} %copy.248, f32[64,128]{1,0:T(8,128)S(1)} %get-tuple-element.192, f32[64,128]{1,0:T(8,128)S(1)} %copy.250, f32[32]{0:T(128)S(1)} %add_multiply_fusion.2, f32[64,128]{1,0:T(8,128)S(1)} %get-tuple-element.194), kind=kOutput, calls=%fused_computation.12.clone.1 | convolution fusion | flops 101974016 | bytes 393344 | tf_op jit(solution)/shard_map/while/body/eval_jaxpr/nyv,nxv->nyx/dot_general | solution.py:42
  122.6 9.1 %fusion.320 = f32[64,32,32]{2,1,0:T(8,128)S(1)} fusion(f32[64,32,32]{2,1,0:T(8,128)S(1)} %fusion.319, f32[32,32]{1,0:T(8,128)S(1)} %copy-done.2, f32[64,128]{1,0:T(8,128)S(1)} %copy.248, f32[64,128]{1,0:T(8,128)S(1)} %get-tuple-element.192, f32[64,128]{1,0:T(8,128)S(1)} %copy.250, f32[32]{0:T(128)S(1)} %add_multiply_fusion.2, ...), kind=kOutput, calls=%fused_computation.18.clone.1 | convolution fusion | flops 102105088 | bytes 659584 | tf_op jit(solution)/shard_map/while/body/eval_jaxpr/nyv,nxv->nyx/dot_general | solution.py:42
  133.0 9.3 %fusion.316 = f32[64,32,32]{2,1,0:T(8,128)S(1)} fusion(f32[64,128]{1,0:T(8,128)S(1)} %copy.248, f32[64,128]{1,0:T(8,128)S(1)} %get-tuple-element.192, f32[64,128]{1,0:T(8,128)S(1)} %copy.250, f32[32]{0:T(128)S(1)} %add_multiply_fusion.2, f32[64,128]{1,0:T(8,128)S(1)} %get-tuple-element.194), kind=kOutput, calls=%fused_computation.11.clone.1 | convolution fusion | flops 101974016 | bytes 393344 | tf_op jit(solution)/shard_map/while/body/eval_jaxpr/nyv,nxv->nyx/dot_general | solution.py:42
  142.2 9.1 %fusion.317 = f32[64,32,32]{2,1,0:T(8,128)S(1)} fusion(f32[64,32,32]{2,1,0:T(8,128)S(1)} %fusion.316, f32[32,32]{1,0:T(8,128)S(1)} %copy-done.2, f32[64,128]{1,0:T(8,128)S(1)} %copy.248, f32[64,128]{1,0:T(8,128)S(1)} %get-tuple-element.192, f32[64,128]{1,0:T(8,128)S(1)} %copy.250, f32[32]{0:T(128)S(1)} %add_multiply_fusion.2, ...), kind=kOutput, calls=%fused_computation.17.clone.1 | convolution fusion | flops 102105088 | bytes 659584 | tf_op jit(solution)/shard_map/while/body/eval_jaxpr/nyv,nxv->nyx/dot_general | solution.py:42
  161.8 8.9 %fusion.319 = f32[64,32,32]{2,1,0:T(8,128)S(1)} fusion(f32[64,128]{1,0:T(8,128)S(1)} %copy.248, f32[64,128]{1,0:T(8,128)S(1)} %get-tuple-element.192, f32[64,128]{1,0:T(8,128)S(1)} %copy.250, f32[32]{0:T(128)S(1)} %add_multiply_fusion.2, f32[64,128]{1,0:T(8,128)S(1)} %get-tuple-element.194), kind=kOutput, calls=%fused_computation.12.clone.1 | convolution fusion | flops 101974016 | bytes 393344 | tf_op jit(solution)/shard_map/while/body/eval_jaxpr/nyv,nxv->nyx/dot_general | solution.py:42
  170.6 9.3 %fusion.320 = f32[64,32,32]{2,1,0:T(8,128)S(1)} fusion(f32[64,32,32]{2,1,0:T(8,128)S(1)} %fusion.319, f32[32,32]{1,0:T(8,128)S(1)} %copy-done.2, f32[64,128]{1,0:T(8,128)S(1)} %copy.248, f32[64,128]{1,0:T(8,128)S(1)} %get-tuple-element.192, f32[64,128]{1,0:T(8,128)S(1)} %copy.250, f32[32]{0:T(128)S(1)} %add_multiply_fusion.2, ...), kind=kOutput, calls=%fused_computation.18.clone.1 | convolution fusion | flops 102105088 | bytes 659584 | tf_op jit(solution)/shard_map/while/body/eval_jaxpr/nyv,nxv->nyx/dot_general | solution.py:42
  181.2 9.0 %fusion.316 = f32[64,32,32]{2,1,0:T(8,128)S(1)} fusion(f32[64,128]{1,0:T(8,128)S(1)} %copy.248, f32[64,128]{1,0:T(8,128)S(1)} %get-tuple-element.192, f32[64,128]{1,0:T(8,128)S(1)} %copy.250, f32[32]{0:T(128)S(1)} %add_multiply_fusion.2, f32[64,128]{1,0:T(8,128)S(1)} %get-tuple-element.194), kind=kOutput, calls=%fused_computation.11.clone.1 | convolution fusion | flops 101974016 | bytes 393344 | tf_op jit(solution)/shard_map/while/body/eval_jaxpr/nyv,nxv->nyx/dot_general | solution.py:42
  190.2 9.1 %fusion.317 = f32[64,32,32]{2,1,0:T(8,128)S(1)} fusion(f32[64,32,32]{2,1,0:T(8,128)S(1)} %fusion.316, f32[32,32]{1,0:T(8,128)S(1)} %copy-done.2, f32[64,128]{1,0:T(8,128)S(1)} %copy.248, f32[64,128]{1,0:T(8,128)S(1)} %get-tuple-element.192, f32[64,128]{1,0:T(8,128)S(1)} %copy.250, f32[32]{0:T(128)S(1)} %add_multiply_fusion.2, ...), kind=kOutput, calls=%fused_computation.17.clone.1 | convolution fusion | flops 102105088 | bytes 659584 | tf_op jit(solution)/shard_map/while/body/eval_jaxpr/nyv,nxv->nyx/dot_general | solution.py:42
  218.4 26.5 %scatter_fusion = f32[512,2,1024]{2,1,0:T(2,128)} fusion(f32[512,2,1024]{2,1,0:T(2,128)} %broadcast_in_dim.11, s32[256]{0:T(256)S(1)} %bitcast.240, f32[256,2,1024]{2,1,0:T(2,128)S(1)} %copy.190), kind=kCustom, calls=%fused_computation.1 | custom fusion | bytes 6292480 | tf_op jit(solution)/shard_map/scatter | solution.py:128
  251.5 7.9 %all-to-all-start.1 = ((f32[16,32,2,1024]{3,2,0,1:T(2,128)}), f32[16,32,2,1024]{3,2,0,1:T(2,128)}, u32[]{:S(2)}, u32[]{:S(2)}) async-start(f32[16,32,2,1024]{3,2,0,1:T(2,128)} %copy.191), calls=%async_computation.1 | async-start | bytes 8388608 | tf_op jit(solution)/shard_map/all_to_all | solution.py:131
  259.6 51.9 %all-to-all-done.1 = f32[16,32,2,1024]{3,2,0,1:T(2,128)} async-done(((f32[16,32,2,1024]{3,2,0,1:T(2,128)}), f32[16,32,2,1024]{3,2,0,1:T(2,128)}, u32[]{:S(2)}, u32[]{:S(2)}) %all-to-all-start.1) | async-done | bytes 4194336 | tf_op jit(solution)/shard_map/all_to_all | solution.py:131
  319.6 8.9 %scatter_custom_fusion.2 = f32[256,2048]{1,0:T(8,128)S(1)} fusion(s32[512]{0:T(512)S(1)} %reshape.227, f32[512,2048]{1,0:T(8,128)} %bitcast.232, f32[]{:T(128)} %constant.129.clone.1), kind=kCustom, calls=%fused_computation.148 | custom fusion | flops 1048576 | bytes 2097664 | tf_op jit(solution)/shard_map/scatter-add | solution.py:137
  333.8 14.3 %copy.211 = f32[2,32,32,8,32]{4,3,0,2,1:T(8,128)} copy(f32[2,32,32,8,32]{4,2,0,3,1:T(8,128)} %bitcast.225) | data formatting | bytes 4194304 | tf_op jit(solution)/shard_map/reshape | solution.py:141
  348.1 7.7 %reshape.240 = f32[2,1024,256]{2,0,1:T(2,128)} reshape(f32[2,32,32,8,32]{4,3,0,2,1:T(8,128)} %copy.211) | data formatting | bytes 4194304 | tf_op jit(solution)/shard_map/reshape | solution.py:141
  355.8 7.4 %all-to-all-start.2 = ((f32[2,1024,256]{2,0,1:T(2,128)}), f32[2,1024,256]{2,0,1:T(2,128)S(1)}, u32[]{:S(2)}, u32[]{:S(2)}) async-start(f32[2,1024,256]{2,0,1:T(2,128)} %reshape.240), calls=%async_computation.2 | async-start | bytes 4194304 | tf_op jit(solution)/shard_map/all_to_all | solution.py:142
  363.3 28.0 %all-to-all-done.2 = f32[2,1024,256]{2,0,1:T(2,128)S(1)} async-done(((f32[2,1024,256]{2,0,1:T(2,128)}), f32[2,1024,256]{2,0,1:T(2,128)S(1)}, u32[]{:S(2)}, u32[]{:S(2)}) %all-to-all-start.2) | async-done | bytes 2097184 | tf_op jit(solution)/shard_map/all_to_all | solution.py:142
  416.0 7.9 %copy.200 = f32[2,32,8192]{1,0,2:T(2,128)} copy(f32[2,32,8192]{2,1,0:T(8,128)S(1)} %pad_maximum_fusion) | data formatting | bytes 4194304 | tf_op jit(solution)/shard_map/stack | solution.py:145
  423.9 10.2 %reshape.246 = f32[32,1,16384]{2,1,0:T(1,128)S(1)} reshape(f32[8192,2,32]{2,1,0:T(2,128)} %bitcast.223) | data formatting | bytes 4194304
  434.1 32.5 %all_to_all.62 = f32[32,1,16384]{2,1,0:T(1,128)} all-to-all(f32[32,1,16384]{2,1,0:T(1,128)S(1)} %reshape.246), channel_id=1, replica_groups=mesh['base'=32,'band'=8] {'base'}, dimensions={0} | all-to-all | bytes 4194304 | tf_op jit(solution)/shard_map/all_to_all | solution.py:144
  474.4 8.4 %reshape.247 = f32[8192,2,32]{2,1,0:T(2,128)} reshape(f32[32,16384]{1,0:T(8,128)S(1)} %reduce.2) | data formatting | bytes 4194304
  482.9 9.7 %copy.213 = f32[2,32,32,256]{3,1,2,0:T(8,128)S(1)} copy(f32[2,32,32,256]{1,0,3,2:T(2,128)} %bitcast.224) | data formatting | bytes 4194304 | tf_op jit(solution)/shard_map/all_to_all | solution.py:144
  494.9 60.2 %all_to_all.63 = f32[2,256,1024]{2,0,1:T(2,128)S(1)} all-to-all(f32[2,256,1024]{2,0,1:T(2,128)} %copy.203), channel_id=1, replica_groups=mesh['base'=32,'band'=8] {'band'}, dimensions={1} | all-to-all | bytes 4194304 | tf_op jit(solution)/shard_map/all_to_all | solution.py:148
  (182 shorter events, 140.0 us)
Async XLA Ops:
  5.8 245.8 %all-to-all-start = ((f32[16,32,1]{0,2,1:T(1,128)}), f32[16,32,1]{0,2,1:T(1,128)S(1)}, u32[]{:S(2)}, u32[]{:S(2)}) async-start(f32[16,32,1]{0,2,1:T(1,128)} %copy.184), calls=%async_computation | async-start | bytes 32768 | tf_op jit(solution)/shard_map/all_to_all | solution.py:132
  15.5 10.8 %copy-start.2 = (f32[32,32]{1,0:T(8,128)S(1)}, f32[32,32]{1,0:T(8,128)}, u32[]{:S(2)}) copy-start(f32[32,32]{1,0:T(8,128)} %get-tuple-element.214) | copy-start | bytes 12292 | tf_op jit(solution)/shard_map/while
  63.8 10.8 %copy-start.2 = (f32[32,32]{1,0:T(8,128)S(1)}, f32[32,32]{1,0:T(8,128)}, u32[]{:S(2)}) copy-start(f32[32,32]{1,0:T(8,128)} %get-tuple-element.214) | copy-start | bytes 12292 | tf_op jit(solution)/shard_map/while
  111.8 10.8 %copy-start.2 = (f32[32,32]{1,0:T(8,128)S(1)}, f32[32,32]{1,0:T(8,128)}, u32[]{:S(2)}) copy-start(f32[32,32]{1,0:T(8,128)} %get-tuple-element.214) | copy-start | bytes 12292 | tf_op jit(solution)/shard_map/while
  159.8 10.8 %copy-start.2 = (f32[32,32]{1,0:T(8,128)S(1)}, f32[32,32]{1,0:T(8,128)}, u32[]{:S(2)}) copy-start(f32[32,32]{1,0:T(8,128)} %get-tuple-element.214) | copy-start | bytes 12292 | tf_op jit(solution)/shard_map/while
  251.5 59.9 %all-to-all-start.1 = ((f32[16,32,2,1024]{3,2,0,1:T(2,128)}), f32[16,32,2,1024]{3,2,0,1:T(2,128)}, u32[]{:S(2)}, u32[]{:S(2)}) async-start(f32[16,32,2,1024]{3,2,0,1:T(2,128)} %copy.191), calls=%async_computation.1 | async-start | bytes 8388608 | tf_op jit(solution)/shard_map/all_to_all | solution.py:131
  355.8 35.6 %all-to-all-start.2 = ((f32[2,1024,256]{2,0,1:T(2,128)}), f32[2,1024,256]{2,0,1:T(2,128)S(1)}, u32[]{:S(2)}, u32[]{:S(2)}) async-start(f32[2,1024,256]{2,0,1:T(2,128)} %reshape.240), calls=%async_computation.2 | async-start | bytes 4194304 | tf_op jit(solution)/shard_map/all_to_all | solution.py:142
  396.4 1.2 copy-start
  560.9 1.2 copy-start.1
where the time goes:
time: 587 us; the launch traced here: 582 us
  matrix products  198 us (34%)
  local copies, waits for them, and re-layouts  156 us (27%)
  blocking collectives  92.6 us (16%)
  waiting for transfers between devices  79.9 us (14%)
  other arithmetic  24.8 us (4%)
  starting transfers between devices  23.8 us (4%)
  loops' own time  6.23 us (1%)
    dot_general x16, matrix products, pairwise(): return jnp.einsum('nyv,nxv->nyx', first_arr, second_arr, precision=exact)  145 us
    all_to_all x1, blocking collectives, shards(): lax.all_to_all(flipped, 'band', split_axis=1, concat_axis=2, tiled=True)  60.2 us
    all_to_all x1, waiting for transfers between devices, shards(): lax.all_to_all(packed, 'base', split_axis=1, concat_axis=1, tiled=True)  51.9 us
    all_to_all x1, blocking collectives, shards(): lax.all_to_all(jnp.stack([row_re, row_im]), 'base', split_axis=2, concat_...  32.5 us
    all_to_all x1, waiting for transfers between devices, shards(): lax.all_to_all(uv_grid, 'base', split_axis=1, concat_axis=2, tiled=True)  28 us
    scatter x1, local copies, waits for them, and re-layouts, shards(): packed = jnp.zeros((buffer_len, 2, area), jnp.float32).at[target].set(tiles)  26.5 us
    unnamed x7, local copies, waits for them, and re-layouts  22.6 us
    reshape x2, local copies, waits for them, and re-layouts, shards(): uv_grid = uv_grid.reshape(2, row_tiles * extent, col_tiles * extent)  22 us
  transfers between devices with their start and end apart: 3, of which 2 were waited for; matrix products, arithmetic and copies ran while one was open for 40% of the time, Pallas kernels for 0%

commit v1 on v0

v1 whole, which is shorter than its diff:
```python
import functools
import math

import jax
import jax.numpy as jnp
import ml_dtypes
import numpy as np
from jax import lax
from jax.experimental import pallas as pl
from jax.experimental.pallas import tpu as pltpu
from jax.sharding import PartitionSpec as P

G = 8192
TILE = 32
SLOT = 256
PAIRS = SLOT // 2
N_BASE = 32
N_BAND = 8
K_TILES = G // TILE
ROWS = PAIRS + 8
F32 = jnp.float32
BF16 = jnp.bfloat16


def split_np(table):
    table = np.asarray(table, np.float64)
    high = table.astype(np.float32).astype(ml_dtypes.bfloat16)
    low = (table - high.astype(np.float64)).astype(np.float32).astype(ml_dtypes.bfloat16)
    return high, low


def waves(first, second, length):
    turns = np.outer(np.asarray(first), np.asarray(second)) % length
    angle = 2.0 * np.pi / length * turns
    return np.cos(angle), np.sin(angle)


def split(x):
    high = x.astype(BF16)
    low = (x - high.astype(F32)).astype(BF16)
    return high, low


def mm(a, b):
    return lax.dot_general(a, b, (((1,), (0,)), ((), ())), preferred_element_type=F32)


def mm_nt(a, b):
    return lax.dot_general(a, b, (((1,), (1,)), ((), ())), preferred_element_type=F32)


def mm3(ah, al, bh, bl):
    return mm(ah, bh) + (mm(al, bh) + mm(ah, bl))


def fit_waves():
    r = 0.5 * np.cos(np.pi * (np.arange(4000) + 0.5) / 4000)
    odd = np.stack([r ** (2 * i + 1) for i in range(7)], 1)
    even = np.stack([r ** (2 * i) for i in range(8)], 1)
    s = np.linalg.lstsq(odd, np.sin(2 * np.pi * r), rcond=None)[0]
    c = np.linalg.lstsq(even, np.cos(2 * np.pi * r), rcond=None)[0]
    return [float(np.float32(v)) for v in s], [float(np.float32(v)) for v in c]


SIN_C, COS_C = fit_waves()


def cos_sin_turns(turns):
    r = turns - jnp.floor(turns + 0.5)
    r2 = r * r
    s = jnp.full_like(r, SIN_C[-1])
    for v in SIN_C[-2::-1]:
        s = s * r2 + v
    c = jnp.full_like(r, COS_C[-1])
    for v in COS_C[-2::-1]:
        c = c * r2 + v
    return c, s * r


UNIT = 8


def powers(base, w8, w16):
    c, s = base
    c8, s8 = w8
    c16, s16 = w16
    return [
        (c * c16 + s * s16, s * c16 - c * s16),
        (c * c8 + s * s8, s * c8 - c * s8),
        (c, s),
        (c * c8 - s * s8, s * c8 + c * s8),
    ]


def grid_kernel(vr_ref, vi_ref, tu_ref, tv_ref, ids_ref, taper_ref, kxh_ref, kxl_ref, fyh_ref, fyl_ref, out_ref, w_ref):
    step8 = lax.broadcasted_iota(jnp.int32, (8, 128), 0).astype(F32)
    lane = lax.broadcasted_iota(jnp.int32, (32, 128), 1)
    for i, ref in enumerate((tu_ref, tv_ref)):
        for j in range(0, SLOT, 64):
            rows = pl.ds(j, 64)
            c8, s8 = cos_sin_turns(ref[rows, :] * 8.0)
            w_ref[4 * i, rows, :] = c8
            w_ref[4 * i + 1, rows, :] = s8
            w_ref[4 * i + 2, rows, :] = c8 * c8 - s8 * s8
            w_ref[4 * i + 3, rows, :] = 2.0 * (c8 * s8)
    pad = jnp.zeros((8, 128), F32)
    ids_pad = jnp.where(lax.broadcasted_iota(jnp.int32, (8, 128), 0) < 2, ids_ref[...], pad)
    for k in range(TILE):
        out_ref[pl.ds(k * ROWS + PAIRS, 8), :] = ids_pad

    def one(s):
        row = pl.ds(s, 1)

        def phases(ref, first):
            turns = ref[row, :] * step8
            w = [jnp.broadcast_to(w_ref[first + i, row, :], (8, 128)) for i in range(4)]
            return powers(cos_sin_turns(turns), (w[0], w[1]), (w[2], w[3]))

        x_side = phases(tu_ref, 0)
        y_side = phases(tv_ref, 4)
        vr = jnp.broadcast_to(vr_ref[row, :], (8, 128))
        vi = jnp.broadcast_to(vi_ref[row, :], (8, 128))
        l_re = jnp.concatenate([vr * c - vi * s for c, s in y_side], 0)
        l_im = jnp.concatenate([vr * s + vi * c for c, s in y_side], 0)
        c_x = jnp.concatenate([c for c, s in x_side], 0)
        s_x = jnp.concatenate([s for c, s in x_side], 0)
        lrh, lrl = split(l_re)
        lih, lil = split(l_im)
        ch, cl = split(c_x)
        sh, sl = split(s_x)
        left = jnp.concatenate([jnp.concatenate([lrh, lih], 1), jnp.concatenate([lrl, lil], 1)], 0)
        right_h = jnp.concatenate([jnp.concatenate([ch, -sh], 1), jnp.concatenate([sh, ch], 1)], 0)
        right_l = jnp.concatenate([jnp.concatenate([cl, -sl], 1), jnp.concatenate([sl, cl], 1)], 0)
        return left, right_h, right_l

    def body(step, carry):
        first = step * UNIT
        pixels = []
        for pair in range(UNIT // 2):
            a, b = one(first + 2 * pair), one(first + 2 * pair + 1)
            left_h = jnp.concatenate([a[0][0:32], b[0][0:32]], 0)
            left_l = jnp.concatenate([a[0][32:64], b[0][32:64]], 0)
            right_h = jnp.concatenate([a[1], b[1]], 0)
            right_l = jnp.concatenate([a[2], b[2]], 0)
            prod = mm_nt(left_h, right_h) + (mm_nt(left_l, right_h) + mm_nt(left_h, right_l))
            pixels.append(jnp.where(lane < 64, prod[0:32], prod[32:64]) * taper_ref[...])
        ph, pl_ = split(jnp.concatenate(pixels, 0))
        q = mm3(ph, pl_, kxh_ref[...], kxl_ref[...])
        for pair in range(UNIT // 2):
            rows = slice(pair * 32, pair * 32 + 32)
            col = jnp.concatenate([q[rows, 0:128], q[rows, 128:256]], 0)
            qh, ql = split(col)
            tile = mm(fyh_ref[...], qh) + (mm(fyl_ref[...], qh) + mm(fyh_ref[...], ql))
            out_ref[pl.ds(step * (UNIT // 2) + pair, 32, stride=ROWS), :] = tile
        return carry

    lax.fori_loop(0, SLOT // UNIT, body, 0)


def grid_tables():
    span = np.arange(TILE)
    c, s = waves(span, span, TILE)
    eye2 = np.eye(2)
    fx = np.block([[c, -s], [s, c]])
    fx_turned = np.block([[-s, -c], [c, -s]])
    kx = np.concatenate([np.kron(eye2, fx), np.kron(eye2, fx_turned)], 1)
    fy = np.concatenate([c, s], 1) / (TILE * math.sqrt(128.0))
    return split_np(kx) + split_np(fy)


def row_kernel(ids_ref, in_ref, eh_ref, el_ref, tc_ref, ts_ref, fh_ref, fl_ref, out_ref, acc_a, acc_b, z_ref):
    def clear(i, carry):
        rows = pl.ds(pl.multiple_of(i * 64, 64), 64)
        acc_a[rows, :] = jnp.zeros((64, 128), F32)
        acc_b[rows, :] = jnp.zeros((64, 128), F32)
        return carry

    lax.fori_loop(0, G // 64, clear, 0)

    def add(i, carry):
        src = i // (PAIRS // 8)
        block = i % (PAIRS // 8)
        base = src * SLOT + block * 8
        rows = in_ref[src, pl.ds(pl.multiple_of(block * 8, 8), 8), :]
        for t in range(8):
            at_a = pl.ds(ids_ref[base + t], 1)
            at_b = pl.ds(ids_ref[base + PAIRS + t], 1)
            acc_a[at_a, :] = acc_a[at_a, :] + rows[t : t + 1]
            acc_b[at_b, :] = acc_b[at_b, :] + rows[t : t + 1]
        return carry

    lax.fori_loop(0, N_BASE * PAIRS // 8, add, 0)

    low_half = lax.broadcasted_iota(jnp.int32, (K_TILES, 128), 1) < 64

    def rows_of(pair, carry):
        one = pl.ds(pl.multiple_of(pair * (2 * K_TILES), K_TILES), K_TILES)
        two = pl.ds(pl.multiple_of(pair * (2 * K_TILES) + K_TILES, K_TILES), K_TILES)
        a1, a2 = acc_a[one, :], acc_a[two, :]
        b1, b2 = acc_b[one, :], acc_b[two, :]
        held = jnp.where(low_half, a1, b2) + pltpu.roll(jnp.where(low_half, a2, b1), 64, 1)
        hh, hl = split(held.T)
        prod = mm3(hh, hl, eh_ref[...], el_ref[...])
        parts = []
        for t in range(2):
            re, im = prod[64 * t : 64 * t + 32], prod[64 * t + 32 : 64 * t + 64]
            y_re = re[:, 0:256] - im[:, 256:512]
            y_im = re[:, 256:512] + im[:, 0:256]
            parts.append(y_re * tc_ref[...] - y_im * ts_ref[...])
            parts.append(y_re * ts_ref[...] + y_im * tc_ref[...])
        vh, vl = split(jnp.concatenate(parts, 0))
        z = mm3(fh_ref[...], fl_ref[...], vh, vl)
        for half in range(2):
            z_ref[half, pl.ds(pl.multiple_of(pair * 128, 128), 128), :] = z[:, 128 * half : 128 * half + 128]
        return carry

    lax.fori_loop(0, TILE // 2, rows_of, 0)

    quarter = lax.broadcasted_iota(jnp.int32, (16, 128), 1) // 32

    def send(b2, carry):
        for half in range(2):
            parts = [z_ref[half, pl.ds(c * 32 + b2, 32, stride=64), :] for c in range(2)]
            pieces = [parts[c][16 * r : 16 * r + 16] for r in range(2) for c in range(2)]
            for zq in range(4):
                block = None
                for p in range(4):
                    moved = pieces[p] if p == zq else pltpu.roll(pieces[p], (p - zq) * 32 % 128, 1)
                    block = moved if block is None else jnp.where(quarter == p, moved, block)
                out_ref[b2 * N_BAND + half * 4 + zq] = block
        return carry

    lax.fori_loop(0, N_BASE, send, 0)


def row_tables():
    span = np.arange(K_TILES)
    c, s = waves(span, span, K_TILES)
    e = np.concatenate([c, s], 1)
    kx = np.arange(TILE)
    tc, ts = waves(kx, span, G)
    c32, s32 = waves(kx, kx, TILE)
    f = np.kron(np.eye(2), np.block([[c32, -s32], [s32, c32]]))
    return split_np(e) + (tc.astype(np.float32), ts.astype(np.float32)) + split_np(f)


def column_kernel(in_ref, eh_ref, el_ref, tc_ref, ts_ref, fh_ref, fl_ref, out_ref, v_ref, x_ref):
    def first(group, carry):
        lefts = []
        for t in range(4):
            block = in_ref[pl.ds((group * 4 + t) * N_BAND, N_BAND)].reshape(128, 128)
            turned = block.T
            lefts.append(jnp.concatenate([turned[0:64], turned[64:128]], 1))
        dh, dl = split(jnp.concatenate(lefts, 0))
        prod = mm3(dh, dl, eh_ref[...], el_ref[...])
        for t in range(4):
            j = group * 4 + t
            re, im = prod[64 * t : 64 * t + 32], prod[64 * t + 32 : 64 * t + 64]
            y_re = re[:, 0:256] - im[:, 256:512]
            y_im = re[:, 256:512] + im[:, 0:256]
            tc = tc_ref[pl.ds(j, 1), :]
            ts = ts_ref[pl.ds(j, 1), :]
            v_re = y_re * tc - y_im * ts
            v_im = y_re * ts + y_im * tc
            for half in range(2):
                lanes = slice(128 * half, 128 * half + 128)
                v_ref[half, pl.ds(j, 32, stride=64), :] = v_re[:, lanes]
                v_ref[half, pl.ds(32 + j, 32, stride=64), :] = v_im[:, lanes]
        return carry

    lax.fori_loop(0, N_BASE // 4, first, 0)

    def second(b, carry):
        rows = pl.ds(pl.multiple_of(b * 64, 64), 64)
        vh, vl = split(jnp.concatenate([v_ref[0, rows, :], v_ref[1, rows, :]], 1))
        x = mm3(fh_ref[...], fl_ref[...], vh, vl)
        for half in range(2):
            x_ref[half, rows, :] = x[:, 128 * half : 128 * half + 128]
        return carry

    lax.fori_loop(0, TILE, second, 0)
    for c in range(2):
        for a2 in range(TILE):
            for half in range(2):
                at = a2 * 256 + half * 128
                out_ref[c, :, at : at + 128] = x_ref[half, pl.ds(c * 32 + a2, 32, stride=64), :]


def column_tables():
    zs, rp, rpp = np.arange(8), np.arange(16), np.arange(2)
    r = (rpp[:, None, None] * 16 + zs[None, :, None] * 32 + rp[None, None, :]).reshape(-1)
    span = np.arange(K_TILES)
    c, s = waves(r, span, K_TILES)
    e = np.concatenate([c, s], 1)
    ky = np.arange(TILE)
    tc, ts = waves(ky, span, G)
    c32, s32 = waves(ky, ky, TILE)
    f = np.block([[c32, -s32], [s32, c32]]) / G
    return split_np(e) + (tc.astype(np.float32), ts.astype(np.float32)) + split_np(f)


VMEM = pl.BlockSpec(memory_space=pltpu.VMEM)
SMEM = pl.BlockSpec(memory_space=pltpu.SMEM)
LIMIT = pltpu.CompilerParams(vmem_limit_bytes=56 * 2**20)


def shards(visibilities, coords, chan_scale, taper_gain, owner_base, tile_cell):
    places = (coords[:, :, :, None] * chan_scale).reshape(SLOT, 2, 128) * (1.0 / TILE)
    ids = (tile_cell // 8) * K_TILES + owner_base[:, 0] * 8 + tile_cell % 8
    ids = ids.reshape(PAIRS, 2).T.astype(F32)
    ids = jnp.concatenate([ids, jnp.zeros((6, PAIRS), F32)], 0)
    taper = jnp.tile(taper_gain, (1, 4))
    sent = pl.pallas_call(
        grid_kernel,
        out_shape=jax.ShapeDtypeStruct((TILE * ROWS, 128), F32),
        in_specs=[VMEM] * 10,
        out_specs=VMEM,
        scratch_shapes=[pltpu.VMEM((8, SLOT, 128), F32)],
        compiler_params=LIMIT,
        name="gridding",
    )(
        visibilities[:, 0, :],
        visibilities[:, 1, :],
        places[:, 0, :],
        places[:, 1, :],
        ids,
        taper,
        *[jnp.asarray(t) for t in grid_tables()],
    )
    arrived = lax.all_to_all(sent.reshape(N_BASE, ROWS, 128), "base", split_axis=0, concat_axis=0, tiled=True)
    where = arrived[:, PAIRS : PAIRS + 2, :].astype(jnp.int32).reshape(N_BASE * SLOT)
    rows = pl.pallas_call(
        row_kernel,
        out_shape=jax.ShapeDtypeStruct((N_BASE * N_BAND, 16, 128), F32),
        in_specs=[SMEM] + [VMEM] * 7,
        out_specs=VMEM,
        scratch_shapes=[
            pltpu.VMEM((G, 128), F32),
            pltpu.VMEM((G, 128), F32),
            pltpu.VMEM((2, TILE * 64, 128), F32),
        ],
        compiler_params=LIMIT,
        name="rows",
    )(where, arrived, *[jnp.asarray(t) for t in row_tables()])
    turned = lax.all_to_all(rows, ("base", "band"), split_axis=0, concat_axis=0, tiled=True)
    return pl.pallas_call(
        column_kernel,
        out_shape=jax.ShapeDtypeStruct((2, TILE, G), F32),
        in_specs=[VMEM] * 7,
        out_specs=VMEM,
        scratch_shapes=[pltpu.VMEM((2, TILE * 64, 128), F32), pltpu.VMEM((2, TILE * 64, 128), F32)],
        compiler_params=LIMIT,
        name="columns",
    )(turned, *[jnp.asarray(t) for t in column_tables()])


def solution(mesh):
    placed = (
        P(("base", "band"), None, None),
        P(("base", "band"), None, None),
        P(),
        P(),
        P(("base", "band"), None),
        P(("base", "band")),
    )
    return jax.shard_map(
        shards,
        mesh=mesh,
        in_specs=placed,
        out_specs=P(None, ("base", "band"), None),
        check_vma=False,
    )
```

time: 587 us -> 195 us (0.33)
  matrix products: 198 us -> 0 us
  local copies, waits for them, and re-layouts: 156 us -> 6.17 us
  Pallas kernels: 0 us -> 82.4 us
  waiting for transfers between devices: 79.9 us -> 0 us
  starting transfers between devices: 23.8 us -> 0 us
  other arithmetic: 24.8 us -> 2.1 us
  blocking collectives: 92.6 us -> 103 us
  loops' own time: 6.23 us -> 0 us
    dot_general x64 -> x0, matrix products: 198 us -> none  [the longest x16 145 us: pairwise(): return jnp.einsum('nyv,nxv->nyx', first_arr, second_arr, precision=exact)]
    pallas_call x0 -> x3, Pallas kernels: none -> 82.4 us  [the longest x1 38.9 us: shards(): pl.pallas_call(row_kernel, out_shape=jax.ShapeDtypeStruct((N_BASE * N_BAN...]
    all_to_all x3 -> x0, waiting for transfers between devices: 79.9 us -> none  [the longest x1 51.9 us: shards(): lax.all_to_all(packed, 'base', split_axis=1, concat_axis=1, tiled=True)]
    reshape x6 -> x0, local copies, waits for them, and re-layouts: 37.8 us -> none  [the longest x2 22 us: shards(): uv_grid = uv_grid.reshape(2, row_tiles * extent, col_tiles * extent)]
    scatter x2 -> x0, local copies, waits for them, and re-layouts: 27.9 us -> none  [the longest x1 26.5 us: shards(): packed = jnp.zeros((buffer_len, 2, area), jnp.float32).at[target].set(tiles)]
    all_to_all x3 -> x0, starting transfers between devices: 23.8 us -> none  [the longest x1 8.59 us: shards(): lax.all_to_all(cell_slots, 'base', split_axis=1, concat_axis=1, tiled=True)]
    unnamed x7 -> x4, local copies, waits for them, and re-layouts: 22.6 us -> 0.72 us
    all_to_all x8 -> x0, local copies, waits for them, and re-layouts: 16.2 us -> none  [the longest x2 10.2 us: shards(): lax.all_to_all(jnp.stack([row_re, row_im]), 'base', split_axis=2, concat_...]
  transfers between devices with their start and end apart: 3 -> 0, of which waited for: 2 -> 0; matrix products, arithmetic and copies ran while one was open for 40% -> 0% of each run, Pallas kernels for 0% -> 0%
where the time goes in v1:
time: 195 us; the launch traced here: 194 us
  blocking collectives  103 us (53%)
  Pallas kernels  82.4 us (42%)
  local copies, waits for them, and re-layouts  6.17 us (3%)
  other arithmetic  2.1 us (1%)
    all_to_all x1, blocking collectives, shards(): lax.all_to_all(rows, ('base', 'band'), split_axis=0, concat_axis=0, tiled...  64.7 us
    pallas_call x1, Pallas kernels, shards(): pl.pallas_call(row_kernel, out_shape=jax.ShapeDtypeStruct((N_BASE * N_BAN...  38.9 us
    all_to_all x1, blocking collectives, shards(): lax.all_to_all(sent.reshape(N_BASE, ROWS, 128), 'base', split_axis=0, con...  38.8 us
    pallas_call x1, Pallas kernels, shards(): pl.pallas_call(grid_kernel, out_shape=jax.ShapeDtypeStruct((TILE * ROWS,...  28.7 us
    pallas_call x1, Pallas kernels, shards(): pl.pallas_call(column_kernel, out_shape=jax.ShapeDtypeStruct((2, TILE, G)...  14.8 us

profile of v1, /device:TPU:1, one launch (start us, length us, event | category | flops | bytes accessed | tf_op | source)
XLA Modules:
  0.0 194.2 jit_solution(17060742015484970017)
XLA Ops:
  0.0 0.0 copy-start.1
  0.0 0.7 broadcast_multiply_fusion
  0.7 0.7 mul.41
  1.4 0.1 mul.42
  1.5 0.7 fusion.1
  2.2 0.1 convert_element_type.13
  2.3 0.1 copy.29
  2.4 0.8 tile.4
  3.1 0.7 tile.10.taper_ref
  3.8 0.7 mul.39
  4.6 0.1 copy.28
  4.7 0.7 slice_bitcast_fusion
  5.4 0.0 copy-done.1
  5.4 0.9 fusion.2
  6.3 0.6 concatenate.3.ids_ref
  6.9 28.7 %gridding.1 = f32[4352,128]{1,0:T(8,128)} custom-call(f32[256,128]{1,0:T(8,128)} %bitcast.18, f32[256,128]{1,0:T(8,128)} %bitcast.17, f32[256,128]{1,0:T(8,128)} %get-tuple-element.6.tu_ref, f32[256,128]{1,0:T(8,128)} %get-tuple-element.5.tv_ref, f32[8,128]{1,0:T(8,128)} %concatenate.3.ids_ref, f32[32,128]{1,0:T(8,128)} %tile.10.taper_ref, ...), custom_call_target="tpu_custom_call" | custom-call | tf_op jit(solution)/shard_map/gridding/pallas_call | solution.py:313
  35.7 38.8 %all_to_all.10.in_ref = f32[32,136,128]{2,1,0:T(8,128)S(1)} all-to-all(f32[32,136,128]{2,1,0:T(8,128)} %bitcast.15), channel_id=1, replica_groups=mesh['base'=32,'band'=8] {'base'}, dimensions={0} | all-to-all | bytes 4456448 | tf_op jit(solution)/shard_map/all_to_all | solution.py:330
  74.4 0.0 copy-start
  74.4 0.7 slice_convert_fusion
  75.1 0.7 copy-done
  75.8 38.9 %rows.1 = f32[256,16,128]{2,1,0:T(8,128)} custom-call(s32[8192]{0:T(1024)} %bitcast.19, f32[32,136,128]{2,1,0:T(8,128)} %copy-done, bf16[256,512]{1,0:T(8,128)(2,1)} %constant.67.clone.eh_ref, bf16[256,512]{1,0:T(8,128)(2,1)} %constant.68.clone.el_ref, f32[32,256]{1,0:T(8,128)} %constant.69.clone.tc_ref, f32[32,256]{1,0:T(8,128)} %constant.70.clone.ts_ref, ...), custom_call_target="tpu_custom_call" | custom-call | tf_op jit(solution)/shard_map/rows/pallas_call | solution.py:332
  114.7 64.7 %all_to_all.11.in_ref = f32[256,16,128]{2,1,0:T(8,128)} all-to-all(f32[256,16,128]{2,1,0:T(8,128)} %rows.1), channel_id=1, replica_groups=mesh['base'=32,'band'=8] {'base','band'}, dimensions={0} | all-to-all | bytes 4194304 | tf_op jit(solution)/shard_map/all_to_all | solution.py:345
  179.4 14.8 %columns.1 = f32[2,32,8192]{2,1,0:T(8,128)} custom-call(f32[256,16,128]{2,1,0:T(8,128)} %all_to_all.11.in_ref, bf16[256,512]{1,0:T(8,128)(2,1)} %constant.73.clone.eh_ref, bf16[256,512]{1,0:T(8,128)(2,1)} %constant.74.clone.el_ref, f32[32,256]{1,0:T(8,128)} %constant.69.clone.tc_ref, f32[32,256]{1,0:T(8,128)} %constant.70.clone.ts_ref, ...), custom_call_target="tpu_custom_call" | custom-call | tf_op jit(solution)/shard_map/columns/pallas_call | solution.py:346
  (1 shorter events, 0.0 us)
Async XLA Ops:
  0.0 5.4 %copy-start.1 = (f32[256,2,128]{2,1,0:T(2,128)S(1)}, f32[256,2,128]{2,1,0:T(2,128)}, u32[]{:S(2)}) copy-start(f32[256,2,128]{2,1,0:T(2,128)} %param.22) | copy-start | bytes 786436
  74.4 1.4 copy-start

commit v2 on v1

--- a/solution.py
+++ b/solution.py
@@ -77,7 +77,9 @@
     return c, s * r
 
 
-UNIT = 8
+UNIT = 32
+CHAINS = 8
+STEP = 64
 
 
 def powers(base, w8, w16):
@@ -168,36 +170,42 @@
     return split_np(kx) + split_np(fy)
 
 
-def row_kernel(ids_ref, in_ref, eh_ref, el_ref, tc_ref, ts_ref, fh_ref, fl_ref, out_ref, acc_a, acc_b, z_ref):
+def row_kernel(ids_ref, in_ref, eh_ref, el_ref, tc_ref, ts_ref, fh_ref, fl_ref, out_ref, z_ref, *accs):
     def clear(i, carry):
         rows = pl.ds(pl.multiple_of(i * 64, 64), 64)
-        acc_a[rows, :] = jnp.zeros((64, 128), F32)
-        acc_b[rows, :] = jnp.zeros((64, 128), F32)
+        for acc in accs:
+            acc[rows, :] = jnp.zeros((64, 128), F32)
         return carry
 
     lax.fori_loop(0, G // 64, clear, 0)
 
     def add(i, carry):
-        src = i // (PAIRS // 8)
-        block = i % (PAIRS // 8)
-        base = src * SLOT + block * 8
-        rows = in_ref[src, pl.ds(pl.multiple_of(block * 8, 8), 8), :]
-        for t in range(8):
-            at_a = pl.ds(ids_ref[base + t], 1)
-            at_b = pl.ds(ids_ref[base + PAIRS + t], 1)
-            acc_a[at_a, :] = acc_a[at_a, :] + rows[t : t + 1]
-            acc_b[at_b, :] = acc_b[at_b, :] + rows[t : t + 1]
-        return carry
-
-    lax.fori_loop(0, N_BASE * PAIRS // 8, add, 0)
+        src = i // (PAIRS // STEP)
+        block = i % (PAIRS // STEP)
+        base = src * SLOT + block * STEP
+        rows = in_ref[src, pl.ds(pl.multiple_of(block * STEP, STEP), STEP), :]
+        for t in range(STEP):
+            for half in range(2):
+                acc = accs[(2 * t + half) % CHAINS]
+                at = pl.ds(ids_ref[base + half * PAIRS + t], 1)
+                acc[at, :] = acc[at, :] + rows[t : t + 1]
+        return carry
+
+    lax.fori_loop(0, N_BASE * PAIRS // STEP, add, 0)
+
+    def total(half, rows):
+        parts = [acc[rows, :] for acc in accs[half::2]]
+        while len(parts) > 1:
+            parts = [x + y for x, y in zip(parts[::2], parts[1::2])]
+        return parts[0]
 
     low_half = lax.broadcasted_iota(jnp.int32, (K_TILES, 128), 1) < 64
 
     def rows_of(pair, carry):
         one = pl.ds(pl.multiple_of(pair * (2 * K_TILES), K_TILES), K_TILES)
         two = pl.ds(pl.multiple_of(pair * (2 * K_TILES) + K_TILES, K_TILES), K_TILES)
-        a1, a2 = acc_a[one, :], acc_a[two, :]
-        b1, b2 = acc_b[one, :], acc_b[two, :]
+        a1, a2 = total(0, one), total(0, two)
+        b1, b2 = total(1, one), total(1, two)
         held = jnp.where(low_half, a1, b2) + pltpu.roll(jnp.where(low_half, a2, b1), 64, 1)
         hh, hl = split(held.T)
         prod = mm3(hh, hl, eh_ref[...], el_ref[...])
@@ -214,7 +222,7 @@
             z_ref[half, pl.ds(pl.multiple_of(pair * 128, 128), 128), :] = z[:, 128 * half : 128 * half + 128]
         return carry
 
-    lax.fori_loop(0, TILE // 2, rows_of, 0)
+    lax.fori_loop(0, TILE // 2, rows_of, 0, unroll=4)
 
     quarter = lax.broadcasted_iota(jnp.int32, (16, 128), 1) // 32
 
@@ -230,7 +238,7 @@
                 out_ref[b2 * N_BAND + half * 4 + zq] = block
         return carry
 
-    lax.fori_loop(0, N_BASE, send, 0)
+    lax.fori_loop(0, N_BASE, send, 0, unroll=4)
 
 
 def row_tables():
@@ -268,7 +276,7 @@
                 v_ref[half, pl.ds(32 + j, 32, stride=64), :] = v_im[:, lanes]
         return carry
 
-    lax.fori_loop(0, N_BASE // 4, first, 0)
+    lax.fori_loop(0, N_BASE // 4, first, 0, unroll=8)
 
     def second(b, carry):
         rows = pl.ds(pl.multiple_of(b * 64, 64), 64)
@@ -278,7 +286,7 @@
             x_ref[half, rows, :] = x[:, 128 * half : 128 * half + 128]
         return carry
 
-    lax.fori_loop(0, TILE, second, 0)
+    lax.fori_loop(0, TILE, second, 0, unroll=16)
     for c in range(2):
         for a2 in range(TILE):
             for half in range(2):
@@ -335,9 +343,8 @@
         in_specs=[SMEM] + [VMEM] * 7,
         out_specs=VMEM,
         scratch_shapes=[
-            pltpu.VMEM((G, 128), F32),
-            pltpu.VMEM((G, 128), F32),
             pltpu.VMEM((2, TILE * 64, 128), F32),
+            *[pltpu.VMEM((G, 128), F32)] * CHAINS,
         ],
         compiler_params=LIMIT,
         name="rows",

time: 195 us -> 163 us (0.84)
  Pallas kernels: 82.4 us -> 50.8 us
    pallas_call x1, Pallas kernels: 38.9 us -> 22.5 us  [shards(): pl.pallas_call(row_kernel, out_shape=jax.ShapeDtypeStruct((N_BASE * N_BAN...]
    pallas_call x1, Pallas kernels: 28.7 us -> 19.3 us  [shards(): pl.pallas_call(grid_kernel, out_shape=jax.ShapeDtypeStruct((TILE * ROWS,...]
    pallas_call x1, Pallas kernels: 14.8 us -> 8.97 us  [shards(): pl.pallas_call(column_kernel, out_shape=jax.ShapeDtypeStruct((2, TILE, G)...]
where the time goes in v2:
time: 163 us
  blocking collectives  103 us (63%)
  Pallas kernels  50.8 us (31%)
  local copies, waits for them, and re-layouts  6.17 us (4%)
  other arithmetic  2.1 us (1%)
    all_to_all x1, blocking collectives, shards(): lax.all_to_all(rows, ('base', 'band'), split_axis=0, concat_axis=0, tiled...  64.7 us
    all_to_all x1, blocking collectives, shards(): lax.all_to_all(sent.reshape(N_BASE, ROWS, 128), 'base', split_axis=0, con...  38.8 us
    pallas_call x1, Pallas kernels, shards(): pl.pallas_call(row_kernel, out_shape=jax.ShapeDtypeStruct((N_BASE * N_BAN...  22.5 us
    pallas_call x1, Pallas kernels, shards(): pl.pallas_call(grid_kernel, out_shape=jax.ShapeDtypeStruct((TILE * ROWS,...  19.3 us
    pallas_call x1, Pallas kernels, shards(): pl.pallas_call(column_kernel, out_shape=jax.ShapeDtypeStruct((2, TILE, G)...  8.97 us

profile of v2, /device:TPU:1, one launch (start us, length us, event | category | flops | bytes accessed | tf_op | source)
XLA Modules:
  0.0 162.5 jit_solution(5274448931618334166)
XLA Ops:
  0.0 0.0 copy-start.1
  0.0 0.7 broadcast_multiply_fusion
  0.7 0.7 mul.41
  1.4 0.1 mul.42
  1.5 0.7 fusion.1
  2.2 0.1 convert_element_type.13
  2.3 0.1 copy.29
  2.4 0.8 tile.4
  3.1 0.7 tile.10.taper_ref
  3.8 0.7 mul.39
  4.6 0.1 copy.28
  4.7 0.7 slice_bitcast_fusion
  5.4 0.0 copy-done.1
  5.4 0.9 fusion.2
  6.3 0.6 concatenate.3.ids_ref
  6.9 19.3 %gridding.1 = f32[4352,128]{1,0:T(8,128)} custom-call(f32[256,128]{1,0:T(8,128)} %bitcast.18, f32[256,128]{1,0:T(8,128)} %bitcast.17, f32[256,128]{1,0:T(8,128)} %get-tuple-element.6.tu_ref, f32[256,128]{1,0:T(8,128)} %get-tuple-element.5.tv_ref, f32[8,128]{1,0:T(8,128)} %concatenate.3.ids_ref, f32[32,128]{1,0:T(8,128)} %tile.10.taper_ref, ...), custom_call_target="tpu_custom_call" | custom-call | tf_op jit(solution)/shard_map/gridding/pallas_call | solution.py:321
  26.2 38.8 %all_to_all.10.in_ref = f32[32,136,128]{2,1,0:T(8,128)S(1)} all-to-all(f32[32,136,128]{2,1,0:T(8,128)} %bitcast.15), channel_id=1, replica_groups=mesh['base'=32,'band'=8] {'base'}, dimensions={0} | all-to-all | bytes 4456448 | tf_op jit(solution)/shard_map/all_to_all | solution.py:338
  65.0 0.0 copy-start
  65.0 0.7 slice_convert_fusion
  65.6 0.7 copy-done
  66.4 22.5 %rows.1 = f32[256,16,128]{2,1,0:T(8,128)} custom-call(s32[8192]{0:T(1024)} %bitcast.19, f32[32,136,128]{2,1,0:T(8,128)} %copy-done, bf16[256,512]{1,0:T(8,128)(2,1)} %constant.67.clone.eh_ref, bf16[256,512]{1,0:T(8,128)(2,1)} %constant.68.clone.el_ref, f32[32,256]{1,0:T(8,128)} %constant.69.clone.tc_ref, f32[32,256]{1,0:T(8,128)} %constant.70.clone.ts_ref, ...), custom_call_target="tpu_custom_call" | custom-call | tf_op jit(solution)/shard_map/rows/pallas_call | solution.py:340
  88.9 64.7 %all_to_all.11.in_ref = f32[256,16,128]{2,1,0:T(8,128)} all-to-all(f32[256,16,128]{2,1,0:T(8,128)} %rows.1), channel_id=1, replica_groups=mesh['base'=32,'band'=8] {'base','band'}, dimensions={0} | all-to-all | bytes 4194304 | tf_op jit(solution)/shard_map/all_to_all | solution.py:352
  153.6 9.0 %columns.1 = f32[2,32,8192]{2,1,0:T(8,128)} custom-call(f32[256,16,128]{2,1,0:T(8,128)} %all_to_all.11.in_ref, bf16[256,512]{1,0:T(8,128)(2,1)} %constant.73.clone.eh_ref, bf16[256,512]{1,0:T(8,128)(2,1)} %constant.74.clone.el_ref, f32[32,256]{1,0:T(8,128)} %constant.69.clone.tc_ref, f32[32,256]{1,0:T(8,128)} %constant.70.clone.ts_ref, ...), custom_call_target="tpu_custom_call" | custom-call | tf_op jit(solution)/shard_map/columns/pallas_call | solution.py:353
  (1 shorter events, 0.0 us)
Async XLA Ops:
  0.0 5.4 %copy-start.1 = (f32[256,2,128]{2,1,0:T(2,128)S(1)}, f32[256,2,128]{2,1,0:T(2,128)}, u32[]{:S(2)}) copy-start(f32[256,2,128]{2,1,0:T(2,128)} %param.22) | copy-start | bytes 786436
  65.0 1.4 copy-start

commit v3 on v2

--- a/solution.py
+++ b/solution.py
@@ -78,6 +78,17 @@
 
 
 UNIT = 32
+SENDS = 4
+MESH = pl.DeviceIdType.MESH
+OFFSETS = sorted(
+    [(x, y, c) for x in range(4) for y in range(4) for c in range(2) if (x, y, c) != (0, 0, 0)],
+    key=lambda d: ((d[0] + d[1]) % 4, d[0], d[2]),
+)
+
+
+def moved(base, offset):
+    x, y, c = base // 8, base // 2 % 4, base % 2
+    return (x + offset[0]) % 4 * 8 + (y + offset[1]) % 4 * 2 + (c + offset[2]) % 2
 CHAINS = 8
 STEP = 64
 
@@ -94,7 +105,11 @@
     ]
 
 
-def grid_kernel(vr_ref, vi_ref, tu_ref, tv_ref, ids_ref, taper_ref, kxh_ref, kxl_ref, fyh_ref, fyl_ref, out_ref, w_ref):
+def grid_kernel(vr_ref, vi_ref, tu_ref, tv_ref, ids_ref, taper_ref, kxh_ref, kxl_ref, fyh_ref, fyl_ref, all_ref, w_ref, out_ref, send_sem, recv_sem, own_sem):
+    base, band = lax.axis_index("base"), lax.axis_index("band")
+    barrier = pltpu.get_barrier_semaphore()
+    for offset in OFFSETS:
+        pl.semaphore_signal(barrier, inc=1, device_id=(moved(base, offset), band), device_id_type=MESH)
     step8 = lax.broadcasted_iota(jnp.int32, (8, 128), 0).astype(F32)
     lane = lax.broadcasted_iota(jnp.int32, (32, 128), 1)
     for i, ref in enumerate((tu_ref, tv_ref)):
@@ -156,7 +171,40 @@
             out_ref[pl.ds(step * (UNIT // 2) + pair, 32, stride=ROWS), :] = tile
         return carry
 
-    lax.fori_loop(0, SLOT // UNIT, body, 0)
+    steps = SLOT // UNIT // SENDS
+
+    def send(part, rows):
+        for offset in OFFSETS:
+            to = moved(base, offset)
+            pltpu.make_async_remote_copy(
+                src_ref=out_ref.at[pl.ds(pl.multiple_of(to * ROWS + part, 8), rows), :],
+                dst_ref=all_ref.at[base, pl.ds(pl.multiple_of(part, 8), rows), :],
+                send_sem=send_sem,
+                recv_sem=recv_sem,
+                device_id=(to, band),
+                device_id_type=MESH,
+            ).start()
+
+    rows = PAIRS // SENDS
+    lax.fori_loop(0, steps, body, 0)
+    pl.semaphore_wait(barrier, len(OFFSETS))
+    send(0, rows)
+
+    def later(part, carry):
+        lax.fori_loop(part * steps, part * steps + steps, body, 0)
+        send(part * rows, rows)
+        return carry
+
+    lax.fori_loop(1, SENDS - 1, later, 0)
+    lax.fori_loop(SLOT // UNIT - steps, SLOT // UNIT, body, 0)
+    send(PAIRS - rows, rows + 8)
+    own = pltpu.make_async_copy(out_ref.at[pl.ds(pl.multiple_of(base * ROWS, 8), ROWS), :], all_ref.at[base], own_sem)
+    own.start()
+    own.wait()
+    sent = out_ref.at[pl.ds(0, len(OFFSETS) * ROWS), :]
+    pltpu.make_async_copy(sent, sent, send_sem).wait()
+    arrived = all_ref.at[pl.ds(0, len(OFFSETS))]
+    pltpu.make_async_copy(arrived, arrived, recv_sem).wait()
 
 
 def grid_tables():
@@ -318,13 +366,19 @@
     ids = ids.reshape(PAIRS, 2).T.astype(F32)
     ids = jnp.concatenate([ids, jnp.zeros((6, PAIRS), F32)], 0)
     taper = jnp.tile(taper_gain, (1, 4))
-    sent = pl.pallas_call(
+    arrived = pl.pallas_call(
         grid_kernel,
-        out_shape=jax.ShapeDtypeStruct((TILE * ROWS, 128), F32),
+        out_shape=jax.ShapeDtypeStruct((N_BASE, ROWS, 128), F32),
         in_specs=[VMEM] * 10,
-        out_specs=VMEM,
-        scratch_shapes=[pltpu.VMEM((8, SLOT, 128), F32)],
-        compiler_params=LIMIT,
+        out_specs=pl.BlockSpec(memory_space=pl.ANY),
+        scratch_shapes=[
+            pltpu.VMEM((8, SLOT, 128), F32),
+            pltpu.VMEM((TILE * ROWS, 128), F32),
+            pltpu.SemaphoreType.DMA,
+            pltpu.SemaphoreType.DMA,
+            pltpu.SemaphoreType.DMA,
+        ],
+        compiler_params=pltpu.CompilerParams(vmem_limit_bytes=56 * 2**20, collective_id=0, has_side_effects=True),
         name="gridding",
     )(
         visibilities[:, 0, :],
@@ -335,7 +389,6 @@
         taper,
         *[jnp.asarray(t) for t in grid_tables()],
     )
-    arrived = lax.all_to_all(sent.reshape(N_BASE, ROWS, 128), "base", split_axis=0, concat_axis=0, tiled=True)
     where = arrived[:, PAIRS : PAIRS + 2, :].astype(jnp.int32).reshape(N_BASE * SLOT)
     rows = pl.pallas_call(
         row_kernel,

time: 163 us -> 141 us (0.87)
  blocking collectives: 103 us -> 64.1 us
  Pallas kernels: 50.8 us -> 68.3 us
    all_to_all x1 -> x0, blocking collectives: 38.8 us -> none  [shards(): lax.all_to_all(sent.reshape(N_BASE, ROWS, 128), 'base', split_axis=0, con...]
    pallas_call x1, Pallas kernels: 19.3 us -> 36.8 us  [shards(): pl.pallas_call(grid_kernel, out_shape=jax.ShapeDtypeStruct((N_BASE, ROWS,...]
where the time goes in v3:
time: 141 us
  Pallas kernels  68.3 us (48%)
  blocking collectives  64.1 us (45%)
  local copies, waits for them, and re-layouts  5.46 us (4%)
  other arithmetic  2.97 us (2%)
    all_to_all x1, blocking collectives, shards(): lax.all_to_all(rows, ('base', 'band'), split_axis=0, concat_axis=0, tiled...  64.1 us
    pallas_call x1, Pallas kernels, shards(): pl.pallas_call(grid_kernel, out_shape=jax.ShapeDtypeStruct((N_BASE, ROWS,...  36.8 us
    pallas_call x1, Pallas kernels, shards(): pl.pallas_call(row_kernel, out_shape=jax.ShapeDtypeStruct((N_BASE * N_BAN...  22.5 us
    pallas_call x1, Pallas kernels, shards(): pl.pallas_call(column_kernel, out_shape=jax.ShapeDtypeStruct((2, TILE, G)...  8.97 us

profile of v3, /device:TPU:1, one launch (start us, length us, event | category | flops | bytes accessed | tf_op | source)
XLA Modules:
  0.0 140.9 jit_solution(11530567480116107400)
XLA Ops:
  0.0 0.0 copy-start
  0.0 0.7 broadcast_multiply_fusion
  0.7 0.7 mul.41
  1.4 0.1 mul.42
  1.5 0.7 fusion.1
  2.2 0.1 convert_element_type.13
  2.3 0.1 copy.29
  2.4 0.8 tile.4
  3.1 0.7 tile.10.taper_ref
  3.8 0.7 mul.39
  4.6 0.1 copy.28
  4.7 0.7 slice_bitcast_fusion
  5.4 0.0 copy-done
  5.4 0.9 fusion.2
  6.3 0.6 concatenate.3.ids_ref
  6.9 36.8 %gridding.1.in_ref = f32[32,136,128]{2,1,0:T(8,128)} custom-call(f32[256,128]{1,0:T(8,128)} %bitcast.16, f32[256,128]{1,0:T(8,128)} %bitcast.15, f32[256,128]{1,0:T(8,128)} %get-tuple-element.6.tu_ref, f32[256,128]{1,0:T(8,128)} %get-tuple-element.5.tv_ref, f32[8,128]{1,0:T(8,128)} %concatenate.3.ids_ref, f32[32,128]{1,0:T(8,128)} %tile.10.taper_ref, ...), custom_call_target="tpu_custom_call" | custom-call | tf_op jit(solution)/shard_map/gridding/pallas_call | solution.py:369
  43.8 1.5 %slice_convert_fusion = s32[32,2,128]{2,1,0:T(2,128)} fusion(f32[32,136,128]{2,1,0:T(8,128)} %gridding.1.in_ref), kind=kLoop, calls=%fused_computation.3 | loop fusion | flops 8192 | bytes 65536 | tf_op jit(solution)/shard_map/convert_element_type | solution.py:392
  45.3 22.5 %rows.1 = f32[256,16,128]{2,1,0:T(8,128)} custom-call(s32[8192]{0:T(1024)} %bitcast.17, f32[32,136,128]{2,1,0:T(8,128)} %gridding.1.in_ref, bf16[256,512]{1,0:T(8,128)(2,1)} %constant.67.clone.eh_ref, bf16[256,512]{1,0:T(8,128)(2,1)} %constant.68.clone.el_ref, f32[32,256]{1,0:T(8,128)} %constant.69.clone.tc_ref, f32[32,256]{1,0:T(8,128)} %constant.70.clone.ts_ref, ...), custom_call_target="tpu_custom_call" | custom-call | tf_op jit(solution)/shard_map/rows/pallas_call | solution.py:393
  67.8 64.1 %all_to_all.5.in_ref = f32[256,16,128]{2,1,0:T(8,128)} all-to-all(f32[256,16,128]{2,1,0:T(8,128)} %rows.1), channel_id=1, replica_groups=mesh['base'=32,'band'=8] {'base','band'}, dimensions={0} | all-to-all | bytes 4194304 | tf_op jit(solution)/shard_map/all_to_all | solution.py:405
  131.9 9.0 %columns.1 = f32[2,32,8192]{2,1,0:T(8,128)} custom-call(f32[256,16,128]{2,1,0:T(8,128)} %all_to_all.5.in_ref, bf16[256,512]{1,0:T(8,128)(2,1)} %constant.73.clone.eh_ref, bf16[256,512]{1,0:T(8,128)(2,1)} %constant.74.clone.el_ref, f32[32,256]{1,0:T(8,128)} %constant.69.clone.tc_ref, f32[32,256]{1,0:T(8,128)} %constant.70.clone.ts_ref, ...), custom_call_target="tpu_custom_call" | custom-call | tf_op jit(solution)/shard_map/columns/pallas_call | solution.py:406
  (1 shorter events, 0.0 us)
Async XLA Ops:
  0.0 5.4 %copy-start = (f32[256,2,128]{2,1,0:T(2,128)S(1)}, f32[256,2,128]{2,1,0:T(2,128)}, u32[]{:S(2)}) copy-start(f32[256,2,128]{2,1,0:T(2,128)} %param.22) | copy-start | bytes 786436

commit v4 on v3

--- a/solution.py
+++ b/solution.py
@@ -105,38 +105,54 @@
     ]
 
 
-def grid_kernel(vr_ref, vi_ref, tu_ref, tv_ref, ids_ref, taper_ref, kxh_ref, kxl_ref, fyh_ref, fyl_ref, all_ref, w_ref, out_ref, send_sem, recv_sem, own_sem):
+def spread(values, table):
+    high = values.astype(BF16)
+    rest = values - high.astype(F32)
+    mid = rest.astype(BF16)
+    low = (rest - mid.astype(F32)).astype(BF16)
+    return mm(high, table) + mm(mid, table) + mm(low, table)
+
+
+def grid_kernel(
+    vis_ref, coords_ref, chan_ref, ids_ref, taper_in_ref, time_ref, chan_at_ref, tile_at_ref,
+    kxh_ref, kxl_ref, fyh_ref, fyl_ref,
+    all_ref, w_ref, out_ref, places_ref, taper_ref, send_sem, recv_sem, own_sem,
+):
     base, band = lax.axis_index("base"), lax.axis_index("band")
     barrier = pltpu.get_barrier_semaphore()
     for offset in OFFSETS:
         pl.semaphore_signal(barrier, inc=1, device_id=(moved(base, offset), band), device_id_type=MESH)
     step8 = lax.broadcasted_iota(jnp.int32, (8, 128), 0).astype(F32)
     lane = lax.broadcasted_iota(jnp.int32, (32, 128), 1)
-    for i, ref in enumerate((tu_ref, tv_ref)):
-        for j in range(0, SLOT, 64):
-            rows = pl.ds(j, 64)
-            c8, s8 = cos_sin_turns(ref[rows, :] * 8.0)
+    taper_ref[...] = spread(taper_in_ref[...], tile_at_ref[...])
+    scale = spread(jnp.broadcast_to(chan_ref[...], (8, 16)), chan_at_ref[...])[0:1] * (1.0 / TILE)
+    for j in range(0, SLOT, 64):
+        rows = pl.ds(j, 64)
+        both = spread(coords_ref[rows, :], time_ref[...])
+        for i in range(2):
+            turns = both[:, 128 * i : 128 * i + 128] * scale
+            places_ref[i, rows, :] = turns
+            c8, s8 = cos_sin_turns(turns * 8.0)
             w_ref[4 * i, rows, :] = c8
             w_ref[4 * i + 1, rows, :] = s8
             w_ref[4 * i + 2, rows, :] = c8 * c8 - s8 * s8
             w_ref[4 * i + 3, rows, :] = 2.0 * (c8 * s8)
-    pad = jnp.zeros((8, 128), F32)
-    ids_pad = jnp.where(lax.broadcasted_iota(jnp.int32, (8, 128), 0) < 2, ids_ref[...], pad)
+    ids_pad = jnp.concatenate([ids_ref[...], jnp.zeros((6, 128), F32)], 0)
     for k in range(TILE):
         out_ref[pl.ds(k * ROWS + PAIRS, 8), :] = ids_pad
 
     def one(s):
         row = pl.ds(s, 1)
 
-        def phases(ref, first):
-            turns = ref[row, :] * step8
+        def phases(side, first):
+            turns = places_ref[side, row, :] * step8
             w = [jnp.broadcast_to(w_ref[first + i, row, :], (8, 128)) for i in range(4)]
             return powers(cos_sin_turns(turns), (w[0], w[1]), (w[2], w[3]))
 
-        x_side = phases(tu_ref, 0)
-        y_side = phases(tv_ref, 4)
-        vr = jnp.broadcast_to(vr_ref[row, :], (8, 128))
-        vi = jnp.broadcast_to(vi_ref[row, :], (8, 128))
+        x_side = phases(0, 0)
+        y_side = phases(1, 4)
+        vr = jnp.broadcast_to(vis_ref[s, 0:1, :], (8, 128))
+        vi = jnp.broadcast_to(vis_ref[s, 1:2, :], (8, 128))
         l_re = jnp.concatenate([vr * c - vi * s for c, s in y_side], 0)
         l_im = jnp.concatenate([vr * s + vi * c for c, s in y_side], 0)
         c_x = jnp.concatenate([c for c, s in x_side], 0)
@@ -151,10 +167,10 @@
         return left, right_h, right_l
 
     def body(step, carry):
-        first = step * UNIT
+        first = step * (UNIT // 2)
         pixels = []
         for pair in range(UNIT // 2):
-            a, b = one(first + 2 * pair), one(first + 2 * pair + 1)
+            a, b = one(first + pair), one(PAIRS + first + pair)
             left_h = jnp.concatenate([a[0][0:32], b[0][0:32]], 0)
             left_l = jnp.concatenate([a[0][32:64], b[0][32:64]], 0)
             right_h = jnp.concatenate([a[1], b[1]], 0)
@@ -168,7 +184,7 @@
             col = jnp.concatenate([q[rows, 0:128], q[rows, 128:256]], 0)
             qh, ql = split(col)
             tile = mm(fyh_ref[...], qh) + (mm(fyl_ref[...], qh) + mm(fyh_ref[...], ql))
-            out_ref[pl.ds(step * (UNIT // 2) + pair, 32, stride=ROWS), :] = tile
+            out_ref[pl.ds(first + pair, 32, stride=ROWS), :] = tile
         return carry
 
     steps = SLOT // UNIT // SENDS
@@ -215,10 +231,15 @@
     fx_turned = np.block([[-s, -c], [c, -s]])
     kx = np.concatenate([np.kron(eye2, fx), np.kron(eye2, fx_turned)], 1)
     fy = np.concatenate([c, s], 1) / (TILE * math.sqrt(128.0))
-    return split_np(kx) + split_np(fy)
-
-
-def row_kernel(ids_ref, in_ref, eh_ref, el_ref, tc_ref, ts_ref, fh_ref, fl_ref, out_ref, z_ref, *accs):
+    q = np.arange(128)
+    time_at = np.equal.outer(np.arange(16), np.concatenate([q // 16, 8 + q // 16]))
+    chan_at = np.equal.outer(np.arange(16), q % 16)
+    tile_at = np.equal.outer(span, q % TILE)
+    ones = tuple(t.astype(np.float32).astype(ml_dtypes.bfloat16) for t in (time_at, chan_at, tile_at))
+    return ones + split_np(kx) + split_np(fy)
+
+
+def row_kernel(ids_ref, in_ref, held_ref, *accs):
     def clear(i, carry):
         rows = pl.ds(pl.multiple_of(i * 64, 64), 64)
         for acc in accs:
@@ -250,43 +271,14 @@
     low_half = lax.broadcasted_iota(jnp.int32, (K_TILES, 128), 1) < 64
 
     def rows_of(pair, carry):
-        one = pl.ds(pl.multiple_of(pair * (2 * K_TILES), K_TILES), K_TILES)
-        two = pl.ds(pl.multiple_of(pair * (2 * K_TILES) + K_TILES, K_TILES), K_TILES)
+        one = pl.ds(pl.multiple_of(pair * K_TILES, K_TILES), K_TILES)
+        two = pl.ds(pl.multiple_of((pair + 16) * K_TILES, K_TILES), K_TILES)
         a1, a2 = total(0, one), total(0, two)
         b1, b2 = total(1, one), total(1, two)
-        held = jnp.where(low_half, a1, b2) + pltpu.roll(jnp.where(low_half, a2, b1), 64, 1)
-        hh, hl = split(held.T)
-        prod = mm3(hh, hl, eh_ref[...], el_ref[...])
-        parts = []
-        for t in range(2):
-            re, im = prod[64 * t : 64 * t + 32], prod[64 * t + 32 : 64 * t + 64]
-            y_re = re[:, 0:256] - im[:, 256:512]
-            y_im = re[:, 256:512] + im[:, 0:256]
-            parts.append(y_re * tc_ref[...] - y_im * ts_ref[...])
-            parts.append(y_re * ts_ref[...] + y_im * tc_ref[...])
-        vh, vl = split(jnp.concatenate(parts, 0))
-        z = mm3(fh_ref[...], fl_ref[...], vh, vl)
-        for half in range(2):
-            z_ref[half, pl.ds(pl.multiple_of(pair * 128, 128), 128), :] = z[:, 128 * half : 128 * half + 128]
-        return carry
-
-    lax.fori_loop(0, TILE // 2, rows_of, 0, unroll=4)
-
-    quarter = lax.broadcasted_iota(jnp.int32, (16, 128), 1) // 32
-
-    def send(b2, carry):
-        for half in range(2):
-            parts = [z_ref[half, pl.ds(c * 32 + b2, 32, stride=64), :] for c in range(2)]
-            pieces = [parts[c][16 * r : 16 * r + 16] for r in range(2) for c in range(2)]
-            for zq in range(4):
-                block = None
-                for p in range(4):
-                    moved = pieces[p] if p == zq else pltpu.roll(pieces[p], (p - zq) * 32 % 128, 1)
-                    block = moved if block is None else jnp.where(quarter == p, moved, block)
-                out_ref[b2 * N_BAND + half * 4 + zq] = block
-        return carry
-
-    lax.fori_loop(0, N_BASE, send, 0, unroll=4)
+        held_ref[one, :] = jnp.where(low_half, a1, b2) + pltpu.roll(jnp.where(low_half, a2, b1), 64, 1)
+        return carry
+
+    lax.fori_loop(0, TILE // 2, rows_of, 0)
 
 
 def row_tables():
@@ -300,32 +292,160 @@
     return split_np(e) + (tc.astype(np.float32), ts.astype(np.float32)) + split_np(f)
 
 
-def column_kernel(in_ref, eh_ref, el_ref, tc_ref, ts_ref, fh_ref, fl_ref, out_ref, v_ref, x_ref):
-    def first(group, carry):
-        lefts = []
-        for t in range(4):
-            block = in_ref[pl.ds((group * 4 + t) * N_BAND, N_BAND)].reshape(128, 128)
-            turned = block.T
-            lefts.append(jnp.concatenate([turned[0:64], turned[64:128]], 1))
-        dh, dl = split(jnp.concatenate(lefts, 0))
-        prod = mm3(dh, dl, eh_ref[...], el_ref[...])
-        for t in range(4):
-            j = group * 4 + t
+TURNS = (2, 1, 3, 0)
+
+
+def wait_for(ref, sem):
+    pltpu.make_async_copy(ref, ref, sem).wait()
+
+
+def send_to(source, target, send_sem, recv_sem, device):
+    pltpu.make_async_remote_copy(
+        src_ref=source,
+        dst_ref=target,
+        send_sem=send_sem,
+        recv_sem=recv_sem,
+        device_id=device,
+        device_id_type=MESH,
+    ).start()
+
+
+def exchange_kernel(
+    held_ref, reh_ref, rel_ref, rtc_ref, rts_ref, rfh_ref, rfl_ref, eh_ref, el_ref, tc_ref, ts_ref,
+    v_ref, z_ref, out_ref, mid_ref, in_ref, send_sem, mid_sem, recv_sem, own_sem,
+):
+    base, band = lax.axis_index("base"), lax.axis_index("band")
+    my_x, my_y, my_core = base // 8, base // 2 % 4, base % 2
+    barrier = pltpu.get_barrier_semaphore()
+    for step in range(1, N_BAND):
+        pl.semaphore_signal(barrier, inc=1, device_id=(base, (band + step) % N_BAND), device_id_type=MESH)
+    for offset in OFFSETS:
+        pl.semaphore_signal(barrier, inc=1, device_id=(moved(base, offset), band), device_id_type=MESH)
+
+    quarter = lax.broadcasted_iota(jnp.int32, (8, 128), 1) // 32
+
+    def transform(pair, carry):
+        hh, hl = split(held_ref[pl.ds(pl.multiple_of(pair * K_TILES, K_TILES), K_TILES), :].T)
+        prod = mm3(hh, hl, reh_ref[...], rel_ref[...])
+        parts = []
+        for t in range(2):
             re, im = prod[64 * t : 64 * t + 32], prod[64 * t + 32 : 64 * t + 64]
             y_re = re[:, 0:256] - im[:, 256:512]
             y_im = re[:, 256:512] + im[:, 0:256]
-            tc = tc_ref[pl.ds(j, 1), :]
-            ts = ts_ref[pl.ds(j, 1), :]
-            v_re = y_re * tc - y_im * ts
-            v_im = y_re * ts + y_im * tc
+            parts.append(y_re * rtc_ref[...] - y_im * rts_ref[...])
+            parts.append(y_re * rts_ref[...] + y_im * rtc_ref[...])
+        vh, vl = split(jnp.concatenate(parts, 0))
+        z = mm3(rfh_ref[...], rfl_ref[...], vh, vl)
+        for half in range(2):
+            z_ref[half, pl.ds(pl.multiple_of(pair * 128, 128), 128), :] = z[:, 128 * half : 128 * half + 128]
+        return carry
+
+    def blocks(part, to_y):
+        def one(i, carry):
+            x, core = i // 2, i % 2
+            b2 = x * 8 + to_y * 2 + core
             for half in range(2):
-                lanes = slice(128 * half, 128 * half + 128)
-                v_ref[half, pl.ds(j, 32, stride=64), :] = v_re[:, lanes]
-                v_ref[half, pl.ds(32 + j, 32, stride=64), :] = v_im[:, lanes]
-        return carry
-
-    lax.fori_loop(0, N_BASE // 4, first, 0, unroll=8)
-
+                pieces = [z_ref[half, pl.ds(part * 1024 + p * 32 + b2, 8, stride=128), :] for p in range(4)]
+                for zq in range(4):
+                    block = None
+                    for p in range(4):
+                        turned = pieces[p] if p == zq else pltpu.roll(pieces[p], (p - zq) * 32 % 128, 1)
+                        block = turned if block is None else jnp.where(quarter == p, turned, block)
+                    out_ref[x, to_y, core, half * 4 + zq, 8 * part : 8 * part + 8, :] = block
+            return carry
+
+        lax.fori_loop(0, 8, one, 0, unroll=4)
+
+    def over_band(part, k):
+        to_y = (my_y + TURNS[k]) % 4
+        rows = pl.ds(8 * part, 8)
+        blocks(part, to_y)
+        if part + k == 0:
+            pl.semaphore_wait(barrier, N_BAND - 1 + len(OFFSETS))
+        for step in (4, 3, 5, 2, 6, 1, 7):
+            to = (band + step) % N_BAND
+            send_to(
+                out_ref.at[:, to_y, :, to, rows, :],
+                mid_ref.at[:, to_y, :, band, rows, :],
+                send_sem,
+                mid_sem.at[4 * part + k],
+                (base, to),
+            )
+        own = pltpu.make_async_copy(
+            out_ref.at[:, to_y, :, band, rows, :], mid_ref.at[:, to_y, :, band, rows, :], own_sem.at[4 * part + k]
+        )
+        own.start()
+        own_mid.append(own)
+
+    def over_base(part, k):
+        to_y = (my_y + TURNS[k]) % 4
+        rows = pl.ds(8 * part, 8)
+        own_mid[4 * part + k].wait()
+        wait_for(out_ref.at[:, 0, :, pl.ds(0, N_BAND - 1), rows, :], mid_sem.at[4 * part + k])
+        for x in range(4):
+            for core in range(2):
+                held = mid_ref.at[(my_x + x) % 4, to_y, (my_core + core) % 2, :, rows, :]
+                target = in_ref.at[base, :, rows, :]
+                if (x, TURNS[k], core) == (0, 0, 0):
+                    own = pltpu.make_async_copy(held, target, own_sem.at[8 + part])
+                    own.start()
+                    own_in.append(own)
+                else:
+                    to = (moved(base, (x, TURNS[k], core)), band)
+                    send_to(held, target, send_sem, recv_sem.at[4 * part + k], to)
+
+    def first(k):
+        for part in range(2):
+            count = 7 if TURNS[k] == 0 else 8
+            wait_for(in_ref.at[pl.ds(0, count), :, pl.ds(8 * part, 8), :], recv_sem.at[4 * part + k])
+            if TURNS[k] == 0:
+                own_in[part].wait()
+        from_y = (my_y - TURNS[k] + 4) % 4
+
+        def group(g, carry):
+            ids = [(2 * g + t // 2) * 8 + from_y * 2 + t % 2 for t in range(4)]
+            lefts = []
+            for j in ids:
+                turned = in_ref[j].reshape(128, 128).T
+                lefts.append(jnp.concatenate([turned[0:64], turned[64:128]], 1))
+            dh, dl = split(jnp.concatenate(lefts, 0))
+            prod = mm3(dh, dl, eh_ref[...], el_ref[...])
+            for t, j in enumerate(ids):
+                re, im = prod[64 * t : 64 * t + 32], prod[64 * t + 32 : 64 * t + 64]
+                y_re = re[:, 0:256] - im[:, 256:512]
+                y_im = re[:, 256:512] + im[:, 0:256]
+                tc = tc_ref[pl.ds(j, 1), :]
+                ts = ts_ref[pl.ds(j, 1), :]
+                v_re = y_re * tc - y_im * ts
+                v_im = y_re * ts + y_im * tc
+                for half in range(2):
+                    lanes = slice(128 * half, 128 * half + 128)
+                    v_ref[half, pl.ds(j, 32, stride=64), :] = v_re[:, lanes]
+                    v_ref[half, pl.ds(32 + j, 32, stride=64), :] = v_im[:, lanes]
+            return carry
+
+        lax.fori_loop(0, 2, group, 0, unroll=2)
+
+    own_mid, own_in = [], []
+    for part in range(2):
+        lax.fori_loop(8 * part, 8 * part + 8, transform, 0, unroll=4)
+        for k in range(4):
+            over_band(part, k)
+    for k in range(4):
+        over_base(0, k)
+    over_base(1, 0)
+    over_base(1, 1)
+    first(0)
+    over_base(1, 2)
+    first(1)
+    over_base(1, 3)
+    first(2)
+    first(3)
+    wait_for(in_ref.at[pl.ds(0, 28)], send_sem)
+    wait_for(in_ref.at[pl.ds(0, 31)], send_sem)
+
+
+def column_kernel(v_ref, fh_ref, fl_ref, out_ref, x_ref):
     def second(b, carry):
         rows = pl.ds(pl.multiple_of(b * 64, 64), 64)
         vh, vl = split(jnp.concatenate([v_ref[0, rows, :], v_ref[1, rows, :]], 1))
@@ -361,19 +481,18 @@
 
 
 def shards(visibilities, coords, chan_scale, taper_gain, owner_base, tile_cell):
-    places = (coords[:, :, :, None] * chan_scale).reshape(SLOT, 2, 128) * (1.0 / TILE)
-    ids = (tile_cell // 8) * K_TILES + owner_base[:, 0] * 8 + tile_cell % 8
-    ids = ids.reshape(PAIRS, 2).T.astype(F32)
-    ids = jnp.concatenate([ids, jnp.zeros((6, PAIRS), F32)], 0)
-    taper = jnp.tile(taper_gain, (1, 4))
+    ids = (tile_cell // 8) * K_TILES + owner_base.reshape(SLOT) * 8 + tile_cell % 8
+    ids = ids.astype(F32).reshape(2, PAIRS)
     arrived = pl.pallas_call(
         grid_kernel,
         out_shape=jax.ShapeDtypeStruct((N_BASE, ROWS, 128), F32),
-        in_specs=[VMEM] * 10,
+        in_specs=[VMEM] * 12,
         out_specs=pl.BlockSpec(memory_space=pl.ANY),
         scratch_shapes=[
             pltpu.VMEM((8, SLOT, 128), F32),
             pltpu.VMEM((TILE * ROWS, 128), F32),
+            pltpu.VMEM((2, SLOT, 128), F32),
+            pltpu.VMEM((TILE, 128), F32),
             pltpu.SemaphoreType.DMA,
             pltpu.SemaphoreType.DMA,
             pltpu.SemaphoreType.DMA,
@@ -381,37 +500,55 @@
         compiler_params=pltpu.CompilerParams(vmem_limit_bytes=56 * 2**20, collective_id=0, has_side_effects=True),
         name="gridding",
     )(
-        visibilities[:, 0, :],
-        visibilities[:, 1, :],
-        places[:, 0, :],
-        places[:, 1, :],
+        visibilities,
+        coords.reshape(SLOT, 16),
+        chan_scale.reshape(1, 16),
         ids,
-        taper,
+        taper_gain,
         *[jnp.asarray(t) for t in grid_tables()],
     )
     where = arrived[:, PAIRS : PAIRS + 2, :].astype(jnp.int32).reshape(N_BASE * SLOT)
+    tables = [jnp.asarray(t) for t in column_tables()]
+    half_rows = pltpu.VMEM((2, TILE * 64, 128), F32)
+    row_side = [jnp.asarray(t) for t in row_tables()]
     rows = pl.pallas_call(
         row_kernel,
-        out_shape=jax.ShapeDtypeStruct((N_BASE * N_BAND, 16, 128), F32),
-        in_specs=[SMEM] + [VMEM] * 7,
+        out_shape=jax.ShapeDtypeStruct((G // 2, 128), F32),
+        in_specs=[SMEM, VMEM],
+        out_specs=VMEM,
+        scratch_shapes=[pltpu.VMEM((G, 128), F32)] * CHAINS,
+        compiler_params=LIMIT,
+        name="rows",
+    )(where, arrived)
+    by_target = pltpu.VMEM((4, 4, 2, N_BAND, 16, 128), F32)
+    dma = pltpu.SemaphoreType.DMA
+    turned = pl.pallas_call(
+        exchange_kernel,
+        out_shape=jax.ShapeDtypeStruct((2, TILE * 64, 128), F32),
+        in_specs=[VMEM] * 11,
         out_specs=VMEM,
         scratch_shapes=[
-            pltpu.VMEM((2, TILE * 64, 128), F32),
-            *[pltpu.VMEM((G, 128), F32)] * CHAINS,
+            half_rows,
+            by_target,
+            by_target,
+            pltpu.VMEM((N_BASE, N_BAND, 16, 128), F32),
+            dma,
+            dma((8,)),
+            dma((8,)),
+            dma((10,)),
         ],
-        compiler_params=LIMIT,
-        name="rows",
-    )(where, arrived, *[jnp.asarray(t) for t in row_tables()])
-    turned = lax.all_to_all(rows, ("base", "band"), split_axis=0, concat_axis=0, tiled=True)
+        compiler_params=pltpu.CompilerParams(vmem_limit_bytes=56 * 2**20, collective_id=1, has_side_effects=True),
+        name="exchange",
+    )(rows, *row_side, *tables[:4])
     return pl.pallas_call(
         column_kernel,
         out_shape=jax.ShapeDtypeStruct((2, TILE, G), F32),
-        in_specs=[VMEM] * 7,
+        in_specs=[VMEM] * 3,
         out_specs=VMEM,
-        scratch_shapes=[pltpu.VMEM((2, TILE * 64, 128), F32), pltpu.VMEM((2, TILE * 64, 128), F32)],
+        scratch_shapes=[half_rows],
         compiler_params=LIMIT,
         name="columns",
-    )(turned, *[jnp.asarray(t) for t in column_tables()])
+    )(turned, *tables[4:])
 
 
 def solution(mesh):

time: 141 us -> 126 us (0.89)
  blocking collectives: 64.1 us -> 0 us
  Pallas kernels: 68.3 us -> 121 us
  local copies, waits for them, and re-layouts: 5.46 us -> 1.47 us
    all_to_all x1 -> x0, blocking collectives: 64.1 us -> none  [shards(): lax.all_to_all(rows, ('base', 'band'), split_axis=0, concat_axis=0, tiled...]
    pallas_call x1 -> x2, Pallas kernels: 22.5 us -> 78.3 us  [the longest x1 63.8 us: shards(): pl.pallas_call(exchange_kernel, out_shape=jax.ShapeDtypeStruct((2, TILE *...]
    pallas_call x1, Pallas kernels: 8.97 us -> 5.27 us  [shards(): pl.pallas_call(column_kernel, out_shape=jax.ShapeDtypeStruct((2, TILE, G)...]
    mul x4 -> x0, local copies, waits for them, and re-layouts: 1.59 us -> none  [shards(): coords[:, :, :, None] * chan_scale]
    reshape x0 -> x1, local copies, waits for them, and re-layouts: none -> 1.47 us  [shards(): coords.reshape(SLOT, 16)]
    another operation x2 -> x0, local copies, waits for them, and re-layouts: 1.45 us -> none  [shards(): taper = jnp.tile(taper_gain, (1, 4))]
where the time goes in v4:
time: 126 us; the launch traced here: 125 us
  Pallas kernels  121 us (96%)
  other arithmetic  3.48 us (3%)
  local copies, waits for them, and re-layouts  1.47 us (1%)
    pallas_call x1, Pallas kernels, shards(): pl.pallas_call(exchange_kernel, out_shape=jax.ShapeDtypeStruct((2, TILE *...  63.8 us
    pallas_call x1, Pallas kernels, shards(): pl.pallas_call(grid_kernel, out_shape=jax.ShapeDtypeStruct((N_BASE, ROWS,...  37 us
    pallas_call x1, Pallas kernels, shards(): pl.pallas_call(row_kernel, out_shape=jax.ShapeDtypeStruct((G // 2, 128),...  14.5 us
    pallas_call x1, Pallas kernels, shards(): pl.pallas_call(column_kernel, out_shape=jax.ShapeDtypeStruct((2, TILE, G)...  5.27 us

profile of v4, /device:TPU:1, one launch (start us, length us, event | category | flops | bytes accessed | tf_op | source)
XLA Modules:
  0.0 125.5 jit_solution(2664751330040354797)
XLA Ops:
  0.0 0.7 broadcast_multiply_fusion
  0.7 1.3 %convert_bitcast_fusion.ids_ref = f32[2,128]{1,0:T(2,128)} fusion(s32[256]{0:T(256)S(1)} %bitcast.8, s32[256]{0:T(256)} %param.30), kind=kLoop, calls=%fused_computation.7 | loop fusion | flops 5888 | bytes 3072 | tf_op jit(solution)/shard_map/reshape | solution.py:485
  2.0 1.5 %copy.27.coords_ref = f32[256,16]{1,0:T(8,128)} copy(f32[256,16]{0,1:T(8,128)} %bitcast.7) | data formatting | bytes 32768 | tf_op jit(solution)/shard_map/reshape | solution.py:504
  3.4 37.0 %gridding.1.in_ref = f32[32,136,128]{2,1,0:T(8,128)} custom-call(f32[256,2,128]{2,1,0:T(2,128)} %vis_ref.1, f32[256,16]{1,0:T(8,128)} %copy.27.coords_ref, f32[1,16]{1,0:T(1,128)} %bitcast.9, f32[2,128]{1,0:T(2,128)} %convert_bitcast_fusion.ids_ref, f32[32,32]{1,0:T(8,128)} %taper_in_ref.1, bf16[16,256]{1,0:T(8,128)(2,1)} %constant.65.clone.time_ref, ...), custom_call_target="tpu_custom_call" | custom-call | tf_op jit(solution)/shard_map/gridding/pallas_call | solution.py:486
  40.4 1.5 %slice_convert_fusion = s32[32,2,128]{2,1,0:T(2,128)} fusion(f32[32,136,128]{2,1,0:T(8,128)} %gridding.1.in_ref), kind=kLoop, calls=%fused_computation | loop fusion | flops 8192 | bytes 65536 | tf_op jit(solution)/shard_map/convert_element_type | solution.py:510
  41.9 14.5 %rows.1.held_ref = f32[4096,128]{1,0:T(8,128)} custom-call(s32[8192]{0:T(1024)} %bitcast.6, f32[32,136,128]{2,1,0:T(8,128)} %gridding.1.in_ref), custom_call_target="tpu_custom_call" | custom-call | tf_op jit(solution)/shard_map/rows/pallas_call | solution.py:514
  56.4 63.8 %exchange.1.v_ref = f32[2,2048,128]{2,1,0:T(8,128)} custom-call(f32[4096,128]{1,0:T(8,128)} %rows.1.held_ref, bf16[256,512]{1,0:T(8,128)(2,1)} %constant.78.clone.reh_ref, bf16[256,512]{1,0:T(8,128)(2,1)} %constant.79.clone.rel_ref, f32[32,256]{1,0:T(8,128)} %constant.74.clone.rtc_ref.tc_ref, f32[32,256]{1,0:T(8,128)} %constant.75.clone.rts_ref.ts_ref, ...), custom_call_target="tpu_custom_call" | custom-call | tf_op jit(solution)/shard_map/exchange/pallas_call | solution.py:525
  120.2 5.3 %columns.1 = f32[2,32,8192]{2,1,0:T(8,128)} custom-call(f32[2,2048,128]{2,1,0:T(8,128)} %exchange.1.v_ref, bf16[64,64]{1,0:T(8,128)(2,1)} %constant.76.clone.fh_ref, bf16[64,64]{1,0:T(8,128)(2,1)} %constant.77.clone.fl_ref), custom_call_target="tpu_custom_call" | custom-call | tf_op jit(solution)/shard_map/columns/pallas_call | solution.py:543

commit v5 on v4

--- a/solution.py
+++ b/solution.py
@@ -78,7 +78,7 @@
 
 
 UNIT = 32
-SENDS = 4
+SENDS = 8
 MESH = pl.DeviceIdType.MESH
 OFFSETS = sorted(
     [(x, y, c) for x in range(4) for y in range(4) for c in range(2) if (x, y, c) != (0, 0, 0)],
@@ -90,7 +90,7 @@
     x, y, c = base // 8, base // 2 % 4, base % 2
     return (x + offset[0]) % 4 * 8 + (y + offset[1]) % 4 * 2 + (c + offset[2]) % 2
 CHAINS = 8
-STEP = 64
+LOADS = 4
 
 
 def powers(base, w8, w16):
@@ -114,7 +114,7 @@
 
 
 def grid_kernel(
-    vis_ref, coords_ref, chan_ref, ids_ref, taper_in_ref, time_ref, chan_at_ref, tile_at_ref,
+    vis_ref, coords_ref, chan_ref, owner_ref, cell_ref, taper_in_ref, time_ref, chan_at_ref, tile_at_ref,
     kxh_ref, kxl_ref, fyh_ref, fyl_ref,
     all_ref, w_ref, out_ref, places_ref, taper_ref, send_sem, recv_sem, own_sem,
 ):
@@ -126,31 +126,23 @@
     lane = lax.broadcasted_iota(jnp.int32, (32, 128), 1)
     taper_ref[...] = spread(taper_in_ref[...], tile_at_ref[...])
     scale = spread(jnp.broadcast_to(chan_ref[...], (8, 16)), chan_at_ref[...])[0:1] * (1.0 / TILE)
-    for j in range(0, SLOT, 64):
-        rows = pl.ds(j, 64)
-        both = spread(coords_ref[rows, :], time_ref[...])
-        for i in range(2):
-            turns = both[:, 128 * i : 128 * i + 128] * scale
-            places_ref[i, rows, :] = turns
-            c8, s8 = cos_sin_turns(turns * 8.0)
-            w_ref[4 * i, rows, :] = c8
-            w_ref[4 * i + 1, rows, :] = s8
-            w_ref[4 * i + 2, rows, :] = c8 * c8 - s8 * s8
-            w_ref[4 * i + 3, rows, :] = 2.0 * (c8 * s8)
-    ids_pad = jnp.concatenate([ids_ref[...], jnp.zeros((6, 128), F32)], 0)
+    cell = cell_ref[...]
+    ids = (cell >> 3) * K_TILES + owner_ref[...] * 8 + (cell & 7)
+    for side in range(2):
+        places_ref[side] = spread(coords_ref[side].T, time_ref[...]) * scale
+    ids_pad = jnp.concatenate([ids.astype(F32), jnp.zeros((6, 128), F32)], 0)
     for k in range(TILE):
         out_ref[pl.ds(k * ROWS + PAIRS, 8), :] = ids_pad
 
     def one(s):
-        row = pl.ds(s, 1)
-
-        def phases(side, first):
+        def phases(side):
+            row = pl.ds(s, 1)
             turns = places_ref[side, row, :] * step8
-            w = [jnp.broadcast_to(w_ref[first + i, row, :], (8, 128)) for i in range(4)]
+            w = [jnp.broadcast_to(w_ref[side, i, row, :], (8, 128)) for i in range(4)]
             return powers(cos_sin_turns(turns), (w[0], w[1]), (w[2], w[3]))
 
-        x_side = phases(0, 0)
-        y_side = phases(1, 4)
+        x_side = phases(0)
+        y_side = phases(1)
         vr = jnp.broadcast_to(vis_ref[s, 0:1, :], (8, 128))
         vi = jnp.broadcast_to(vis_ref[s, 1:2, :], (8, 128))
         l_re = jnp.concatenate([vr * c - vi * s for c, s in y_side], 0)
@@ -168,6 +160,14 @@
 
     def body(step, carry):
         first = step * (UNIT // 2)
+        for half in range(2):
+            rows = pl.ds(pl.multiple_of(half * PAIRS + first, UNIT // 2), UNIT // 2)
+            for side in range(2):
+                c8, s8 = cos_sin_turns(places_ref[side, rows, :] * 8.0)
+                w_ref[side, 0, rows, :] = c8
+                w_ref[side, 1, rows, :] = s8
+                w_ref[side, 2, rows, :] = c8 * c8 - s8 * s8
+                w_ref[side, 3, rows, :] = 2.0 * (c8 * s8)
         pixels = []
         for pair in range(UNIT // 2):
             a, b = one(first + pair), one(PAIRS + first + pair)
@@ -232,14 +232,30 @@
     kx = np.concatenate([np.kron(eye2, fx), np.kron(eye2, fx_turned)], 1)
     fy = np.concatenate([c, s], 1) / (TILE * math.sqrt(128.0))
     q = np.arange(128)
-    time_at = np.equal.outer(np.arange(16), np.concatenate([q // 16, 8 + q // 16]))
+    time_at = np.equal.outer(np.arange(8), q // 16)
     chan_at = np.equal.outer(np.arange(16), q % 16)
     tile_at = np.equal.outer(span, q % TILE)
     ones = tuple(t.astype(np.float32).astype(ml_dtypes.bfloat16) for t in (time_at, chan_at, tile_at))
     return ones + split_np(kx) + split_np(fy)
 
 
-def row_kernel(ids_ref, in_ref, held_ref, *accs):
+def row_kernel(all_ref, held_ref, in_ref, out_ref, number_ref, where_ref, ids_ref, load_sem, store_sem, ids_sem, *accs):
+    numbers = pltpu.make_async_copy(all_ref.at[:, pl.ds(PAIRS, 8), :], number_ref, ids_sem)
+    numbers.start()
+    sources = N_BASE // LOADS
+    loads = []
+    for i in range(LOADS):
+        part = pl.ds(i * sources, sources)
+        loads.append(
+            pltpu.make_async_copy(all_ref.at[part, pl.ds(0, PAIRS), :], in_ref.at[part], load_sem.at[i])
+        )
+        loads[i].start()
+    numbers.wait()
+    for src in range(N_BASE):
+        where_ref[2 * src : 2 * src + 2, :] = number_ref[src, 0:2, :].astype(jnp.int32)
+    ids_copy = pltpu.make_async_copy(where_ref, ids_ref, ids_sem)
+    ids_copy.start()
+
     def clear(i, carry):
         rows = pl.ds(pl.multiple_of(i * 64, 64), 64)
         for acc in accs:
@@ -247,20 +263,20 @@
         return carry
 
     lax.fori_loop(0, G // 64, clear, 0)
-
-    def add(i, carry):
-        src = i // (PAIRS // STEP)
-        block = i % (PAIRS // STEP)
-        base = src * SLOT + block * STEP
-        rows = in_ref[src, pl.ds(pl.multiple_of(block * STEP, STEP), STEP), :]
-        for t in range(STEP):
+    ids_copy.wait()
+
+    def add(src, carry):
+        for t in range(PAIRS):
+            row = in_ref[src, t : t + 1, :]
             for half in range(2):
                 acc = accs[(2 * t + half) % CHAINS]
-                at = pl.ds(ids_ref[base + half * PAIRS + t], 1)
-                acc[at, :] = acc[at, :] + rows[t : t + 1]
+                at = pl.ds(ids_ref[2 * src + half, t], 1)
+                acc[at, :] = acc[at, :] + row
         return carry
 
-    lax.fori_loop(0, N_BASE * PAIRS // STEP, add, 0)
+    for i in range(LOADS):
+        loads[i].wait()
+        lax.fori_loop(i * sources, (i + 1) * sources, add, 0)
 
     def total(half, rows):
         parts = [acc[rows, :] for acc in accs[half::2]]
@@ -275,10 +291,18 @@
         two = pl.ds(pl.multiple_of((pair + 16) * K_TILES, K_TILES), K_TILES)
         a1, a2 = total(0, one), total(0, two)
         b1, b2 = total(1, one), total(1, two)
-        held_ref[one, :] = jnp.where(low_half, a1, b2) + pltpu.roll(jnp.where(low_half, a2, b1), 64, 1)
+        out_ref[one, :] = jnp.where(low_half, a1, b2) + pltpu.roll(jnp.where(low_half, a2, b1), 64, 1)
         return carry
 
-    lax.fori_loop(0, TILE // 2, rows_of, 0)
+    stores = []
+    pairs = 16 // LOADS
+    for i in range(LOADS):
+        lax.fori_loop(i * pairs, (i + 1) * pairs, rows_of, 0, unroll=2)
+        part = pl.ds(i * pairs * K_TILES, pairs * K_TILES)
+        stores.append(pltpu.make_async_copy(out_ref.at[part, :], held_ref.at[part, :], store_sem.at[i]))
+        stores[i].start()
+    for store in stores:
+        store.wait()
 
 
 def row_tables():
@@ -311,11 +335,16 @@
 
 
 def exchange_kernel(
-    held_ref, reh_ref, rel_ref, rtc_ref, rts_ref, rfh_ref, rfl_ref, eh_ref, el_ref, tc_ref, ts_ref,
-    v_ref, z_ref, out_ref, mid_ref, in_ref, send_sem, mid_sem, recv_sem, own_sem,
+    rows_ref, reh_ref, rel_ref, rtc_ref, rts_ref, rfh_ref, rfl_ref, eh_ref, el_ref, tc_ref, ts_ref,
+    v_ref, held_ref, z_ref, out_ref, mid_ref, in_ref, load_sem, send_sem, mid_sem, recv_sem, own_sem,
 ):
     base, band = lax.axis_index("base"), lax.axis_index("band")
     my_x, my_y, my_core = base // 8, base // 2 % 4, base % 2
+    loads = []
+    for i in range(4):
+        part = pl.ds(i * 4 * K_TILES, 4 * K_TILES)
+        loads.append(pltpu.make_async_copy(rows_ref.at[part, :], held_ref.at[part, :], load_sem.at[i]))
+        loads[i].start()
     barrier = pltpu.get_barrier_semaphore()
     for step in range(1, N_BAND):
         pl.semaphore_signal(barrier, inc=1, device_id=(base, (band + step) % N_BAND), device_id_type=MESH)
@@ -428,7 +457,9 @@
 
     own_mid, own_in = [], []
     for part in range(2):
-        lax.fori_loop(8 * part, 8 * part + 8, transform, 0, unroll=4)
+        for i in range(2 * part, 2 * part + 2):
+            loads[i].wait()
+            lax.fori_loop(4 * i, 4 * i + 4, transform, 0, unroll=4)
         for k in range(4):
             over_band(part, k)
     for k in range(4):
@@ -454,12 +485,12 @@
             x_ref[half, rows, :] = x[:, 128 * half : 128 * half + 128]
         return carry
 
-    lax.fori_loop(0, TILE, second, 0, unroll=16)
+    lax.fori_loop(0, 8, second, 0, unroll=8)
     for c in range(2):
         for a2 in range(TILE):
             for half in range(2):
                 at = a2 * 256 + half * 128
-                out_ref[c, :, at : at + 128] = x_ref[half, pl.ds(c * 32 + a2, 32, stride=64), :]
+                out_ref[c, :, at : at + 128] = x_ref[half, pl.ds(c * 32 + a2, 8, stride=64), :]
 
 
 def column_tables():
@@ -476,20 +507,18 @@
 
 
 VMEM = pl.BlockSpec(memory_space=pltpu.VMEM)
-SMEM = pl.BlockSpec(memory_space=pltpu.SMEM)
+HBM = pl.BlockSpec(memory_space=pl.ANY)
 LIMIT = pltpu.CompilerParams(vmem_limit_bytes=56 * 2**20)
 
 
 def shards(visibilities, coords, chan_scale, taper_gain, owner_base, tile_cell):
-    ids = (tile_cell // 8) * K_TILES + owner_base.reshape(SLOT) * 8 + tile_cell % 8
-    ids = ids.astype(F32).reshape(2, PAIRS)
     arrived = pl.pallas_call(
         grid_kernel,
         out_shape=jax.ShapeDtypeStruct((N_BASE, ROWS, 128), F32),
-        in_specs=[VMEM] * 12,
+        in_specs=[VMEM] * 13,
         out_specs=pl.BlockSpec(memory_space=pl.ANY),
         scratch_shapes=[
-            pltpu.VMEM((8, SLOT, 128), F32),
+            pltpu.VMEM((2, 4, SLOT, 128), F32),
             pltpu.VMEM((TILE * ROWS, 128), F32),
             pltpu.VMEM((2, SLOT, 128), F32),
             pltpu.VMEM((TILE, 128), F32),
@@ -501,37 +530,49 @@
         name="gridding",
     )(
         visibilities,
-        coords.reshape(SLOT, 16),
+        coords.transpose(1, 2, 0),
         chan_scale.reshape(1, 16),
-        ids,
+        owner_base.reshape(2, PAIRS),
+        tile_cell.reshape(2, PAIRS),
         taper_gain,
         *[jnp.asarray(t) for t in grid_tables()],
     )
-    where = arrived[:, PAIRS : PAIRS + 2, :].astype(jnp.int32).reshape(N_BASE * SLOT)
     tables = [jnp.asarray(t) for t in column_tables()]
     half_rows = pltpu.VMEM((2, TILE * 64, 128), F32)
     row_side = [jnp.asarray(t) for t in row_tables()]
     rows = pl.pallas_call(
         row_kernel,
         out_shape=jax.ShapeDtypeStruct((G // 2, 128), F32),
-        in_specs=[SMEM, VMEM],
-        out_specs=VMEM,
-        scratch_shapes=[pltpu.VMEM((G, 128), F32)] * CHAINS,
+        in_specs=[HBM],
+        out_specs=HBM,
+        scratch_shapes=[
+            pltpu.VMEM((N_BASE, PAIRS, 128), F32),
+            pltpu.VMEM((G // 2, 128), F32),
+            pltpu.VMEM((N_BASE, 8, 128), F32),
+            pltpu.VMEM((2 * N_BASE, PAIRS), jnp.int32),
+            pltpu.SMEM((2 * N_BASE, PAIRS), jnp.int32),
+            pltpu.SemaphoreType.DMA((LOADS,)),
+            pltpu.SemaphoreType.DMA((LOADS,)),
+            pltpu.SemaphoreType.DMA,
+            *[pltpu.VMEM((G, 128), F32)] * CHAINS,
+        ],
         compiler_params=LIMIT,
         name="rows",
-    )(where, arrived)
+    )(arrived)
     by_target = pltpu.VMEM((4, 4, 2, N_BAND, 16, 128), F32)
     dma = pltpu.SemaphoreType.DMA
     turned = pl.pallas_call(
         exchange_kernel,
         out_shape=jax.ShapeDtypeStruct((2, TILE * 64, 128), F32),
-        in_specs=[VMEM] * 11,
+        in_specs=[HBM] + [VMEM] * 10,
         out_specs=VMEM,
         scratch_shapes=[
+            pltpu.VMEM((G // 2, 128), F32),
             half_rows,
             by_target,
             by_target,
             pltpu.VMEM((N_BASE, N_BAND, 16, 128), F32),
+            dma((4,)),
             dma,
             dma((8,)),
             dma((8,)),
@@ -543,9 +584,14 @@
     return pl.pallas_call(
         column_kernel,
         out_shape=jax.ShapeDtypeStruct((2, TILE, G), F32),
-        in_specs=[VMEM] * 3,
-        out_specs=VMEM,
-        scratch_shapes=[half_rows],
+        grid=(TILE // 8,),
+        in_specs=[
+            pl.BlockSpec((2, 512, 128), lambda i: (0, i, 0)),
+            pl.BlockSpec((64, 64), lambda i: (0, 0)),
+            pl.BlockSpec((64, 64), lambda i: (0, 0)),
+        ],
+        out_specs=pl.BlockSpec((2, 8, G), lambda i: (0, i, 0)),
+        scratch_shapes=[pltpu.VMEM((2, 512, 128), F32)],
         compiler_params=LIMIT,
         name="columns",
     )(turned, *tables[4:])

time: 126 us -> 118 us (0.937)
  other arithmetic: 3.48 us -> 0 us
  Pallas kernels: 121 us -> 118 us
  local copies, waits for them, and re-layouts: 1.47 us -> 0 us
    pallas_call x1, Pallas kernels: 37 us -> 34.8 us  [shards(): pl.pallas_call(grid_kernel, out_shape=jax.ShapeDtypeStruct((N_BASE, ROWS,...]
    pallas_call x1, Pallas kernels: 63.8 us -> 65.7 us  [shards(): pl.pallas_call(exchange_kernel, out_shape=jax.ShapeDtypeStruct((2, TILE *...]
    pallas_call x1, Pallas kernels: 14.5 us -> 12.7 us  [shards(): pl.pallas_call(row_kernel, out_shape=jax.ShapeDtypeStruct((G // 2, 128),...]
    convert_element_type x1 -> x0, other arithmetic: 1.52 us -> none  [shards(): arrived[:, PAIRS:PAIRS + 2, :].astype(jnp.int32).reshape(N_BASE * SLOT)]
    reshape x1 -> x0, local copies, waits for them, and re-layouts: 1.47 us -> none  [shards(): coords.reshape(SLOT, 16)]
    reshape x1 -> x0, other arithmetic: 1.28 us -> none  [shards(): ids = ids.astype(F32).reshape(2, PAIRS)]
where the time goes in v5:
time: 118 us
  Pallas kernels  118 us (100%)
    pallas_call x1, Pallas kernels, shards(): pl.pallas_call(exchange_kernel, out_shape=jax.ShapeDtypeStruct((2, TILE *...  65.7 us
    pallas_call x1, Pallas kernels, shards(): pl.pallas_call(grid_kernel, out_shape=jax.ShapeDtypeStruct((N_BASE, ROWS,...  34.8 us
    pallas_call x1, Pallas kernels, shards(): pl.pallas_call(row_kernel, out_shape=jax.ShapeDtypeStruct((G // 2, 128),...  12.7 us
    pallas_call x1, Pallas kernels, shards(): pl.pallas_call(column_kernel, out_shape=jax.ShapeDtypeStruct((2, TILE, G)...  5.01 us

profile of v5, /device:TPU:1, one launch (start us, length us, event | category | flops | bytes accessed | tf_op | source)
XLA Modules:
  0.0 118.3 jit_solution(18348125972496202324)
XLA Ops:
  0.0 34.8 %gridding.1.all_ref = f32[32,136,128]{2,1,0:T(8,128)} custom-call(f32[256,2,128]{2,1,0:T(2,128)} %vis_ref.1, f32[2,8,256]{2,1,0:T(8,128)} %bitcast.4, f32[1,16]{1,0:T(1,128)} %bitcast.7, s32[2,128]{1,0:T(2,128)} %bitcast.5, s32[2,128]{1,0:T(2,128)} %bitcast.6, f32[32,32]{1,0:T(8,128)} %taper_in_ref.1, bf16[8,128]{1,0:T(8,128)(2,1)} %constant.34.clone.time_ref, ...), custom_call_target="tpu_custom_call" | custom-call | tf_op jit(solution)/shard_map/gridding/pallas_call | solution.py:515
  34.8 12.7 %rows.1.rows_ref = f32[4096,128]{1,0:T(8,128)} custom-call(f32[32,136,128]{2,1,0:T(8,128)} %gridding.1.all_ref), custom_call_target="tpu_custom_call" | custom-call | tf_op jit(solution)/shard_map/rows/pallas_call | solution.py:543
  47.5 65.7 %exchange.1.v_ref = f32[2,2048,128]{2,1,0:T(8,128)} custom-call(f32[4096,128]{1,0:T(8,128)} %rows.1.rows_ref, bf16[256,512]{1,0:T(8,128)(2,1)} %constant.47.clone.reh_ref, bf16[256,512]{1,0:T(8,128)(2,1)} %constant.48.clone.rel_ref, f32[32,256]{1,0:T(8,128)} %constant.43.clone.rtc_ref.tc_ref, f32[32,256]{1,0:T(8,128)} %constant.44.clone.rts_ref.ts_ref, ...), custom_call_target="tpu_custom_call" | custom-call | tf_op jit(solution)/shard_map/exchange/pallas_call | solution.py:564
  113.2 5.0 %columns.1 = f32[2,32,8192]{2,1,0:T(8,128)} custom-call(f32[2,2048,128]{2,1,0:T(8,128)} %exchange.1.v_ref, bf16[64,64]{1,0:T(8,128)(2,1)} %constant.45.clone.fh_ref, bf16[64,64]{1,0:T(8,128)(2,1)} %constant.46.clone.fl_ref), custom_call_target="tpu_custom_call" | custom-call | tf_op jit(solution)/shard_map/columns/pallas_call | solution.py:584

commit v6 on v5

--- a/solution.py
+++ b/solution.py
@@ -50,7 +50,9 @@
 
 
 def mm3(ah, al, bh, bl):
-    return mm(ah, bh) + (mm(al, bh) + mm(ah, bl))
+    rows = ah.shape[0]
+    both = mm(jnp.concatenate([ah, al], 0), bh)
+    return both[:rows] + (both[rows:] + mm(ah, bl))
 
 
 def fit_waves():
@@ -89,6 +91,8 @@
 def moved(base, offset):
     x, y, c = base // 8, base // 2 % 4, base % 2
     return (x + offset[0]) % 4 * 8 + (y + offset[1]) % 4 * 2 + (c + offset[2]) % 2
+PITCH = 72
+Z_PITCH = 136
 CHAINS = 8
 LOADS = 4
 
@@ -116,7 +120,7 @@
 def grid_kernel(
     vis_ref, coords_ref, chan_ref, owner_ref, cell_ref, taper_in_ref, time_ref, chan_at_ref, tile_at_ref,
     kxh_ref, kxl_ref, fyh_ref, fyl_ref,
-    all_ref, w_ref, out_ref, places_ref, taper_ref, send_sem, recv_sem, own_sem,
+    all_ref, all_ids_ref, w_ref, out_ref, ids_ref, places_ref, taper_ref, send_sem, recv_sem, own_sem,
 ):
     base, band = lax.axis_index("base"), lax.axis_index("band")
     barrier = pltpu.get_barrier_semaphore()
@@ -127,13 +131,9 @@
     taper_ref[...] = spread(taper_in_ref[...], tile_at_ref[...])
     scale = spread(jnp.broadcast_to(chan_ref[...], (8, 16)), chan_at_ref[...])[0:1] * (1.0 / TILE)
     cell = cell_ref[...]
-    ids = (cell >> 3) * K_TILES + owner_ref[...] * 8 + (cell & 7)
+    ids_ref[...] = (cell >> 3) * K_TILES + owner_ref[...] * 8 + (cell & 7)
     for side in range(2):
         places_ref[side] = spread(coords_ref[side].T, time_ref[...]) * scale
-    ids_pad = jnp.concatenate([ids.astype(F32), jnp.zeros((6, 128), F32)], 0)
-    for k in range(TILE):
-        out_ref[pl.ds(k * ROWS + PAIRS, 8), :] = ids_pad
-
     def one(s):
         def phases(side):
             row = pl.ds(s, 1)
@@ -175,7 +175,8 @@
             left_l = jnp.concatenate([a[0][32:64], b[0][32:64]], 0)
             right_h = jnp.concatenate([a[1], b[1]], 0)
             right_l = jnp.concatenate([a[2], b[2]], 0)
-            prod = mm_nt(left_h, right_h) + (mm_nt(left_l, right_h) + mm_nt(left_h, right_l))
+            both = mm_nt(jnp.concatenate([left_h, left_l], 0), right_h)
+            prod = both[0:64] + (both[64:128] + mm_nt(left_h, right_l))
             pixels.append(jnp.where(lane < 64, prod[0:32], prod[32:64]) * taper_ref[...])
         ph, pl_ = split(jnp.concatenate(pixels, 0))
         q = mm3(ph, pl_, kxh_ref[...], kxl_ref[...])
@@ -183,7 +184,7 @@
             rows = slice(pair * 32, pair * 32 + 32)
             col = jnp.concatenate([q[rows, 0:128], q[rows, 128:256]], 0)
             qh, ql = split(col)
-            tile = mm(fyh_ref[...], qh) + (mm(fyl_ref[...], qh) + mm(fyh_ref[...], ql))
+            tile = mm3(fyh_ref[...], fyl_ref[...], qh, ql)
             out_ref[pl.ds(first + pair, 32, stride=ROWS), :] = tile
         return carry
 
@@ -195,8 +196,8 @@
             pltpu.make_async_remote_copy(
                 src_ref=out_ref.at[pl.ds(pl.multiple_of(to * ROWS + part, 8), rows), :],
                 dst_ref=all_ref.at[base, pl.ds(pl.multiple_of(part, 8), rows), :],
-                send_sem=send_sem,
-                recv_sem=recv_sem,
+                send_sem=send_sem.at[0],
+                recv_sem=recv_sem.at[0],
                 device_id=(to, band),
                 device_id_type=MESH,
             ).start()
@@ -205,6 +206,15 @@
     lax.fori_loop(0, steps, body, 0)
     pl.semaphore_wait(barrier, len(OFFSETS))
     send(0, rows)
+    for offset in OFFSETS:
+        pltpu.make_async_remote_copy(
+            src_ref=ids_ref,
+            dst_ref=all_ids_ref.at[base],
+            send_sem=send_sem.at[1],
+            recv_sem=recv_sem.at[1],
+            device_id=(moved(base, offset), band),
+            device_id_type=MESH,
+        ).start()
 
     def later(part, carry):
         lax.fori_loop(part * steps, part * steps + steps, body, 0)
@@ -213,14 +223,21 @@
 
     lax.fori_loop(1, SENDS - 1, later, 0)
     lax.fori_loop(SLOT // UNIT - steps, SLOT // UNIT, body, 0)
-    send(PAIRS - rows, rows + 8)
-    own = pltpu.make_async_copy(out_ref.at[pl.ds(pl.multiple_of(base * ROWS, 8), ROWS), :], all_ref.at[base], own_sem)
-    own.start()
-    own.wait()
-    sent = out_ref.at[pl.ds(0, len(OFFSETS) * ROWS), :]
-    pltpu.make_async_copy(sent, sent, send_sem).wait()
-    arrived = all_ref.at[pl.ds(0, len(OFFSETS))]
-    pltpu.make_async_copy(arrived, arrived, recv_sem).wait()
+    send(PAIRS - rows, rows)
+    own = [
+        pltpu.make_async_copy(
+            out_ref.at[pl.ds(pl.multiple_of(base * ROWS, 8), PAIRS), :], all_ref.at[base], own_sem.at[0]
+        ),
+        pltpu.make_async_copy(ids_ref, all_ids_ref.at[base], own_sem.at[1]),
+    ]
+    for copy in own:
+        copy.start()
+    for copy in own:
+        copy.wait()
+    for i, ref in enumerate((all_ref, all_ids_ref)):
+        arrived = ref.at[pl.ds(0, len(OFFSETS))]
+        pltpu.make_async_copy(arrived, arrived, send_sem.at[i]).wait()
+        pltpu.make_async_copy(arrived, arrived, recv_sem.at[i]).wait()
 
 
 def grid_tables():
@@ -239,23 +256,17 @@
     return ones + split_np(kx) + split_np(fy)
 
 
-def row_kernel(all_ref, held_ref, in_ref, out_ref, number_ref, where_ref, ids_ref, load_sem, store_sem, ids_sem, *accs):
-    numbers = pltpu.make_async_copy(all_ref.at[:, pl.ds(PAIRS, 8), :], number_ref, ids_sem)
-    numbers.start()
+def row_kernel(all_ref, all_ids_ref, held_ref, in_ref, out_ref, ids_ref, load_sem, store_sem, ids_sem, *accs):
+    ids_copy = pltpu.make_async_copy(all_ids_ref, ids_ref, ids_sem)
+    ids_copy.start()
     sources = N_BASE // LOADS
     loads = []
     for i in range(LOADS):
         part = pl.ds(i * sources, sources)
         loads.append(
-            pltpu.make_async_copy(all_ref.at[part, pl.ds(0, PAIRS), :], in_ref.at[part], load_sem.at[i])
+            pltpu.make_async_copy(all_ref.at[part], in_ref.at[part], load_sem.at[i])
         )
         loads[i].start()
-    numbers.wait()
-    for src in range(N_BASE):
-        where_ref[2 * src : 2 * src + 2, :] = number_ref[src, 0:2, :].astype(jnp.int32)
-    ids_copy = pltpu.make_async_copy(where_ref, ids_ref, ids_sem)
-    ids_copy.start()
-
     def clear(i, carry):
         rows = pl.ds(pl.multiple_of(i * 64, 64), 64)
         for acc in accs:
@@ -270,7 +281,7 @@
             row = in_ref[src, t : t + 1, :]
             for half in range(2):
                 acc = accs[(2 * t + half) % CHAINS]
-                at = pl.ds(ids_ref[2 * src + half, t], 1)
+                at = pl.ds(ids_ref[src, half, t], 1)
                 acc[at, :] = acc[at, :] + row
         return carry
 
@@ -312,7 +323,7 @@
     kx = np.arange(TILE)
     tc, ts = waves(kx, span, G)
     c32, s32 = waves(kx, kx, TILE)
-    f = np.kron(np.eye(2), np.block([[c32, -s32], [s32, c32]]))
+    f = np.kron(np.eye(4), np.block([[c32, -s32], [s32, c32]]))
     return split_np(e) + (tc.astype(np.float32), ts.astype(np.float32)) + split_np(f)
 
 
@@ -353,28 +364,32 @@
 
     quarter = lax.broadcasted_iota(jnp.int32, (8, 128), 1) // 32
 
-    def transform(pair, carry):
-        hh, hl = split(held_ref[pl.ds(pl.multiple_of(pair * K_TILES, K_TILES), K_TILES), :].T)
+    def transform(group):
+        turned = [held_ref[pl.ds((4 * group + i) * K_TILES, K_TILES), :].T for i in range(4)]
+        hh, hl = split(jnp.concatenate(turned, 0))
         prod = mm3(hh, hl, reh_ref[...], rel_ref[...])
-        parts = []
-        for t in range(2):
-            re, im = prod[64 * t : 64 * t + 32], prod[64 * t + 32 : 64 * t + 64]
-            y_re = re[:, 0:256] - im[:, 256:512]
-            y_im = re[:, 256:512] + im[:, 0:256]
-            parts.append(y_re * rtc_ref[...] - y_im * rts_ref[...])
-            parts.append(y_re * rts_ref[...] + y_im * rtc_ref[...])
-        vh, vl = split(jnp.concatenate(parts, 0))
-        z = mm3(rfh_ref[...], rfl_ref[...], vh, vl)
-        for half in range(2):
-            z_ref[half, pl.ds(pl.multiple_of(pair * 128, 128), 128), :] = z[:, 128 * half : 128 * half + 128]
-        return carry
+        for i in range(2):
+            parts = []
+            for t in range(4):
+                at = 256 * i + 64 * t
+                re, im = prod[at : at + 32], prod[at + 32 : at + 64]
+                y_re = re[:, 0:256] - im[:, 256:512]
+                y_im = re[:, 256:512] + im[:, 0:256]
+                parts.append(y_re * rtc_ref[...] - y_im * rts_ref[...])
+                parts.append(y_re * rts_ref[...] + y_im * rtc_ref[...])
+            vh, vl = split(jnp.concatenate(parts, 0))
+            z = mm3(rfh_ref[...], rfl_ref[...], vh, vl)
+            for half in range(2):
+                for j in range(2):
+                    at = pl.ds((4 * group + 2 * i + j) * Z_PITCH, 128)
+                    z_ref[half, at, :] = z[128 * j : 128 * j + 128, 128 * half : 128 * half + 128]
 
     def blocks(part, to_y):
         def one(i, carry):
             x, core = i // 2, i % 2
             b2 = x * 8 + to_y * 2 + core
             for half in range(2):
-                pieces = [z_ref[half, pl.ds(part * 1024 + p * 32 + b2, 8, stride=128), :] for p in range(4)]
+                pieces = [z_ref[half, pl.ds(part * 8 * Z_PITCH + p * 32 + b2, 8, stride=Z_PITCH), :] for p in range(4)]
                 for zq in range(4):
                     block = None
                     for p in range(4):
@@ -391,75 +406,75 @@
         blocks(part, to_y)
         if part + k == 0:
             pl.semaphore_wait(barrier, N_BAND - 1 + len(OFFSETS))
-        for step in (4, 3, 5, 2, 6, 1, 7):
-            to = (band + step) % N_BAND
-            send_to(
-                out_ref.at[:, to_y, :, to, rows, :],
-                mid_ref.at[:, to_y, :, band, rows, :],
-                send_sem,
-                mid_sem.at[4 * part + k],
-                (base, to),
-            )
-        own = pltpu.make_async_copy(
-            out_ref.at[:, to_y, :, band, rows, :], mid_ref.at[:, to_y, :, band, rows, :], own_sem.at[4 * part + k]
-        )
-        own.start()
-        own_mid.append(own)
-
-    def over_base(part, k):
+        groups = ((slice(None),),) if (part, k) != (1, 3) else (tuple((my_x + x) % 4 for x in (2, 1, 3)), (my_x,))
+        for i, columns in enumerate(groups):
+            sem = 4 * part + k + i
+            for step in (4, 3, 5, 2, 6, 1, 7, 0):
+                to = (band + step) % N_BAND
+                for x in columns:
+                    source = out_ref.at[x, to_y, :, to, rows, :]
+                    target = mid_ref.at[x, to_y, :, band, rows, :]
+                    if step:
+                        send_to(source, target, send_sem, mid_sem.at[sem], (base, to))
+                    else:
+                        own_mid[sem].append(pltpu.make_async_copy(source, target, own_sem.at[len(started)]))
+                        own_mid[sem][-1].start()
+                        started.append(sem)
+
+    def over_base(part, k, own_chip=None):
         to_y = (my_y + TURNS[k]) % 4
         rows = pl.ds(8 * part, 8)
-        own_mid[4 * part + k].wait()
-        wait_for(out_ref.at[:, 0, :, pl.ds(0, N_BAND - 1), rows, :], mid_sem.at[4 * part + k])
-        for x in range(4):
+        sem = 4 * part + k + int(bool(own_chip))
+        for own in own_mid[sem]:
+            own.wait()
+        count = {None: 4, False: 3, True: 1}[own_chip]
+        wait_for(out_ref.at[pl.ds(0, count), 0, :, pl.ds(0, N_BAND - 1), rows, :], mid_sem.at[sem])
+        for x in {None: range(4), False: (2, 1, 3), True: (0,)}[own_chip]:
             for core in range(2):
                 held = mid_ref.at[(my_x + x) % 4, to_y, (my_core + core) % 2, :, rows, :]
                 target = in_ref.at[base, :, rows, :]
                 if (x, TURNS[k], core) == (0, 0, 0):
-                    own = pltpu.make_async_copy(held, target, own_sem.at[8 + part])
+                    own = pltpu.make_async_copy(held, target, own_sem.at[11 + part])
                     own.start()
                     own_in.append(own)
                 else:
                     to = (moved(base, (x, TURNS[k], core)), band)
-                    send_to(held, target, send_sem, recv_sem.at[4 * part + k], to)
+                    send_to(held, target, send_sem, recv_sem.at[sem], to)
 
     def first(k):
         for part in range(2):
-            count = 7 if TURNS[k] == 0 else 8
-            wait_for(in_ref.at[pl.ds(0, count), :, pl.ds(8 * part, 8), :], recv_sem.at[4 * part + k])
+            for i, count in enumerate(((8,), (7,), (6, 1))[0 if TURNS[k] else 1 + part]):
+                came = in_ref.at[pl.ds(0, count), :, pl.ds(8 * part, 8), :]
+                wait_for(came, recv_sem.at[4 * part + k + i])
             if TURNS[k] == 0:
                 own_in[part].wait()
         from_y = (my_y - TURNS[k] + 4) % 4
 
-        def group(g, carry):
-            ids = [(2 * g + t // 2) * 8 + from_y * 2 + t % 2 for t in range(4)]
-            lefts = []
-            for j in ids:
-                turned = in_ref[j].reshape(128, 128).T
-                lefts.append(jnp.concatenate([turned[0:64], turned[64:128]], 1))
-            dh, dl = split(jnp.concatenate(lefts, 0))
-            prod = mm3(dh, dl, eh_ref[...], el_ref[...])
-            for t, j in enumerate(ids):
-                re, im = prod[64 * t : 64 * t + 32], prod[64 * t + 32 : 64 * t + 64]
-                y_re = re[:, 0:256] - im[:, 256:512]
-                y_im = re[:, 256:512] + im[:, 0:256]
-                tc = tc_ref[pl.ds(j, 1), :]
-                ts = ts_ref[pl.ds(j, 1), :]
-                v_re = y_re * tc - y_im * ts
-                v_im = y_re * ts + y_im * tc
-                for half in range(2):
-                    lanes = slice(128 * half, 128 * half + 128)
-                    v_ref[half, pl.ds(j, 32, stride=64), :] = v_re[:, lanes]
-                    v_ref[half, pl.ds(32 + j, 32, stride=64), :] = v_im[:, lanes]
-            return carry
-
-        lax.fori_loop(0, 2, group, 0, unroll=2)
-
-    own_mid, own_in = [], []
+        ids = [t // 2 * 8 + from_y * 2 + t % 2 for t in range(8)]
+        lefts = []
+        for j in ids:
+            turned = in_ref[j].reshape(128, 128).T
+            lefts.append(jnp.concatenate([turned[0:64], turned[64:128]], 1))
+        dh, dl = split(jnp.concatenate(lefts, 0))
+        prod = mm3(dh, dl, eh_ref[...], el_ref[...])
+        for t, j in enumerate(ids):
+            re, im = prod[64 * t : 64 * t + 32], prod[64 * t + 32 : 64 * t + 64]
+            y_re = re[:, 0:256] - im[:, 256:512]
+            y_im = re[:, 256:512] + im[:, 0:256]
+            tc = tc_ref[pl.ds(j, 1), :]
+            ts = ts_ref[pl.ds(j, 1), :]
+            v_re = y_re * tc - y_im * ts
+            v_im = y_re * ts + y_im * tc
+            for half in range(2):
+                lanes = slice(128 * half, 128 * half + 128)
+                v_ref[half, pl.ds(j, 32, stride=PITCH), :] = v_re[:, lanes]
+                v_ref[half, pl.ds(32 + j, 32, stride=PITCH), :] = v_im[:, lanes]
+
+    own_mid, own_in, started = [[] for _ in range(9)], [], []
     for part in range(2):
         for i in range(2 * part, 2 * part + 2):
             loads[i].wait()
-            lax.fori_loop(4 * i, 4 * i + 4, transform, 0, unroll=4)
+            transform(i)
         for k in range(4):
             over_band(part, k)
     for k in range(4):
@@ -469,28 +484,26 @@
     first(0)
     over_base(1, 2)
     first(1)
-    over_base(1, 3)
+    over_base(1, 3, False)
     first(2)
+    over_base(1, 3, True)
     first(3)
     wait_for(in_ref.at[pl.ds(0, 28)], send_sem)
     wait_for(in_ref.at[pl.ds(0, 31)], send_sem)
 
 
 def column_kernel(v_ref, fh_ref, fl_ref, out_ref, x_ref):
-    def second(b, carry):
-        rows = pl.ds(pl.multiple_of(b * 64, 64), 64)
+    for i in range(8):
+        rows = pl.ds(PITCH * i, 64)
         vh, vl = split(jnp.concatenate([v_ref[0, rows, :], v_ref[1, rows, :]], 1))
         x = mm3(fh_ref[...], fl_ref[...], vh, vl)
         for half in range(2):
             x_ref[half, rows, :] = x[:, 128 * half : 128 * half + 128]
-        return carry
-
-    lax.fori_loop(0, 8, second, 0, unroll=8)
     for c in range(2):
         for a2 in range(TILE):
             for half in range(2):
                 at = a2 * 256 + half * 128
-                out_ref[c, :, at : at + 128] = x_ref[half, pl.ds(c * 32 + a2, 8, stride=64), :]
+                out_ref[c, :, at : at + 128] = x_ref[half, pl.ds(c * 32 + a2, 8, stride=PITCH), :]
 
 
 def column_tables():
@@ -512,19 +525,23 @@
 
 
 def shards(visibilities, coords, chan_scale, taper_gain, owner_base, tile_cell):
-    arrived = pl.pallas_call(
+    arrived, ids = pl.pallas_call(
         grid_kernel,
-        out_shape=jax.ShapeDtypeStruct((N_BASE, ROWS, 128), F32),
+        out_shape=(
+            jax.ShapeDtypeStruct((N_BASE, PAIRS, 128), F32),
+            jax.ShapeDtypeStruct((N_BASE, 2, PAIRS), jnp.int32),
+        ),
         in_specs=[VMEM] * 13,
-        out_specs=pl.BlockSpec(memory_space=pl.ANY),
+        out_specs=(HBM, HBM),
         scratch_shapes=[
             pltpu.VMEM((2, 4, SLOT, 128), F32),
             pltpu.VMEM((TILE * ROWS, 128), F32),
+            pltpu.VMEM((2, PAIRS), jnp.int32),
             pltpu.VMEM((2, SLOT, 128), F32),
             pltpu.VMEM((TILE, 128), F32),
-            pltpu.SemaphoreType.DMA,
-            pltpu.SemaphoreType.DMA,
-            pltpu.SemaphoreType.DMA,
+            pltpu.SemaphoreType.DMA((2,)),
+            pltpu.SemaphoreType.DMA((2,)),
+            pltpu.SemaphoreType.DMA((2,)),
         ],
         compiler_params=pltpu.CompilerParams(vmem_limit_bytes=56 * 2**20, collective_id=0, has_side_effects=True),
         name="gridding",
@@ -538,19 +555,16 @@
         *[jnp.asarray(t) for t in grid_tables()],
     )
     tables = [jnp.asarray(t) for t in column_tables()]
-    half_rows = pltpu.VMEM((2, TILE * 64, 128), F32)
     row_side = [jnp.asarray(t) for t in row_tables()]
     rows = pl.pallas_call(
         row_kernel,
         out_shape=jax.ShapeDtypeStruct((G // 2, 128), F32),
-        in_specs=[HBM],
+        in_specs=[HBM, HBM],
         out_specs=HBM,
         scratch_shapes=[
             pltpu.VMEM((N_BASE, PAIRS, 128), F32),
             pltpu.VMEM((G // 2, 128), F32),
-            pltpu.VMEM((N_BASE, 8, 128), F32),
-            pltpu.VMEM((2 * N_BASE, PAIRS), jnp.int32),
-            pltpu.SMEM((2 * N_BASE, PAIRS), jnp.int32),
+            pltpu.SMEM((N_BASE, 2, PAIRS), jnp.int32),
             pltpu.SemaphoreType.DMA((LOADS,)),
             pltpu.SemaphoreType.DMA((LOADS,)),
             pltpu.SemaphoreType.DMA,
@@ -558,25 +572,25 @@
         ],
         compiler_params=LIMIT,
         name="rows",
-    )(arrived)
+    )(arrived, ids)
     by_target = pltpu.VMEM((4, 4, 2, N_BAND, 16, 128), F32)
     dma = pltpu.SemaphoreType.DMA
     turned = pl.pallas_call(
         exchange_kernel,
-        out_shape=jax.ShapeDtypeStruct((2, TILE * 64, 128), F32),
+        out_shape=jax.ShapeDtypeStruct((2, TILE * PITCH, 128), F32),
         in_specs=[HBM] + [VMEM] * 10,
         out_specs=VMEM,
         scratch_shapes=[
             pltpu.VMEM((G // 2, 128), F32),
-            half_rows,
+            pltpu.VMEM((2, 16 * Z_PITCH, 128), F32),
             by_target,
             by_target,
             pltpu.VMEM((N_BASE, N_BAND, 16, 128), F32),
             dma((4,)),
             dma,
-            dma((8,)),
-            dma((8,)),
-            dma((10,)),
+            dma((9,)),
+            dma((9,)),
+            dma((13,)),
         ],
         compiler_params=pltpu.CompilerParams(vmem_limit_bytes=56 * 2**20, collective_id=1, has_side_effects=True),
         name="exchange",
@@ -586,12 +600,12 @@
         out_shape=jax.ShapeDtypeStruct((2, TILE, G), F32),
         grid=(TILE // 8,),
         in_specs=[
-            pl.BlockSpec((2, 512, 128), lambda i: (0, i, 0)),
+            pl.BlockSpec((2, 8 * PITCH, 128), lambda i: (0, i, 0)),
             pl.BlockSpec((64, 64), lambda i: (0, 0)),
             pl.BlockSpec((64, 64), lambda i: (0, 0)),
         ],
         out_specs=pl.BlockSpec((2, 8, G), lambda i: (0, i, 0)),
-        scratch_shapes=[pltpu.VMEM((2, 512, 128), F32)],
+        scratch_shapes=[pltpu.VMEM((2, 8 * PITCH, 128), F32)],
         compiler_params=LIMIT,
         name="columns",
     )(turned, *tables[4:])

time: 118 us -> 114 us (0.966)
  Pallas kernels: 118 us -> 113 us
    pallas_call x1, Pallas kernels: 65.7 us -> 63.8 us  [shards(): pl.pallas_call(exchange_kernel, out_shape=jax.ShapeDtypeStruct((2, TILE *...]
    pallas_call x1, Pallas kernels: 12.7 us -> 11.3 us  [shards(): pl.pallas_call(row_kernel, out_shape=jax.ShapeDtypeStruct((G // 2, 128),...]
where the time goes in v6:
time: 114 us; the launch traced here: 113 us
  Pallas kernels  113 us (99%)
    pallas_call x1, Pallas kernels, shards(): pl.pallas_call(exchange_kernel, out_shape=jax.ShapeDtypeStruct((2, TILE *...  63.8 us
    pallas_call x1, Pallas kernels, shards(): pl.pallas_call(grid_kernel, out_shape=(jax.ShapeDtypeStruct((N_BASE, PAIR...  33.6 us
    pallas_call x1, Pallas kernels, shards(): pl.pallas_call(row_kernel, out_shape=jax.ShapeDtypeStruct((G // 2, 128),...  11.3 us
    pallas_call x1, Pallas kernels, shards(): pl.pallas_call(column_kernel, out_shape=jax.ShapeDtypeStruct((2, TILE, G)...  4.62 us

profile of v6, /device:TPU:1, one launch (start us, length us, event | category | flops | bytes accessed | tf_op | source)
XLA Modules:
  0.0 113.4 jit_solution(1356604324352014719)
XLA Ops:
  0.0 33.6 %gridding.1 = (f32[32,128,128]{2,1,0:T(8,128)}, s32[32,2,128]{2,1,0:T(2,128)}) custom-call(f32[256,2,128]{2,1,0:T(2,128)} %vis_ref.1, f32[2,8,256]{2,1,0:T(8,128)} %bitcast.4, f32[1,16]{1,0:T(1,128)} %bitcast.7, s32[2,128]{1,0:T(2,128)} %bitcast.5, s32[2,128]{1,0:T(2,128)} %bitcast.6, f32[32,32]{1,0:T(8,128)} %taper_in_ref.1, ...), custom_call_target="tpu_custom_call" | custom-call | tf_op jit(solution)/shard_map/gridding/pallas_call | solution.py:528
  33.6 11.3 %rows.1.rows_ref = f32[4096,128]{1,0:T(8,128)} custom-call(f32[32,128,128]{2,1,0:T(8,128)} %get-tuple-element.7.all_ref, s32[32,2,128]{2,1,0:T(2,128)} %get-tuple-element.8.all_ids_ref), custom_call_target="tpu_custom_call" | custom-call | tf_op jit(solution)/shard_map/rows/pallas_call | solution.py:559
  45.0 63.8 %exchange.1.v_ref = f32[2,2304,128]{2,1,0:T(8,128)} custom-call(f32[4096,128]{1,0:T(8,128)} %rows.1.rows_ref, bf16[256,512]{1,0:T(8,128)(2,1)} %constant.47.clone.reh_ref, bf16[256,512]{1,0:T(8,128)(2,1)} %constant.48.clone.rel_ref, f32[32,256]{1,0:T(8,128)} %constant.43.clone.rtc_ref.tc_ref, f32[32,256]{1,0:T(8,128)} %constant.44.clone.rts_ref.ts_ref, ...), custom_call_target="tpu_custom_call" | custom-call | tf_op jit(solution)/shard_map/exchange/pallas_call | solution.py:578
  108.8 4.6 %columns.1 = f32[2,32,8192]{2,1,0:T(8,128)} custom-call(f32[2,2304,128]{2,1,0:T(8,128)} %exchange.1.v_ref, bf16[64,64]{1,0:T(8,128)(2,1)} %constant.45.clone.fh_ref, bf16[64,64]{1,0:T(8,128)(2,1)} %constant.46.clone.fl_ref), custom_call_target="tpu_custom_call" | custom-call | tf_op jit(solution)/shard_map/columns/pallas_call | solution.py:598

commit v7 on v6

--- a/solution.py
+++ b/solution.py
@@ -328,6 +328,7 @@
 
 
 TURNS = (2, 1, 3, 0)
+FAR = (2, 1, 3)
 
 
 def wait_for(ref, sem):
@@ -406,35 +407,40 @@
         blocks(part, to_y)
         if part + k == 0:
             pl.semaphore_wait(barrier, N_BAND - 1 + len(OFFSETS))
-        groups = ((slice(None),),) if (part, k) != (1, 3) else (tuple((my_x + x) % 4 for x in (2, 1, 3)), (my_x,))
-        for i, columns in enumerate(groups):
-            sem = 4 * part + k + i
-            for step in (4, 3, 5, 2, 6, 1, 7, 0):
-                to = (band + step) % N_BAND
-                for x in columns:
-                    source = out_ref.at[x, to_y, :, to, rows, :]
-                    target = mid_ref.at[x, to_y, :, band, rows, :]
-                    if step:
-                        send_to(source, target, send_sem, mid_sem.at[sem], (base, to))
-                    else:
-                        own_mid[sem].append(pltpu.make_async_copy(source, target, own_sem.at[len(started)]))
-                        own_mid[sem][-1].start()
-                        started.append(sem)
-
-    def over_base(part, k, own_chip=None):
+        if k < 3:
+            band_copies(4 * part + k, (slice(None),), to_y, rows)
+        else:
+            band_copies(4 * part + k, [(my_x + x) % 4 for x in FAR], to_y, rows)
+        if (part, k) == (1, 3):
+            band_copies(8, (my_x,), to_y, pl.ds(0, 16))
+
+    def band_copies(sem, columns, to_y, rows):
+        for step in (4, 3, 5, 2, 6, 1, 7, 0):
+            to = (band + step) % N_BAND
+            for x in columns:
+                source = out_ref.at[x, to_y, :, to, rows, :]
+                target = mid_ref.at[x, to_y, :, band, rows, :]
+                if step:
+                    send_to(source, target, send_sem, mid_sem.at[sem], (base, to))
+                else:
+                    own_mid[sem].append(pltpu.make_async_copy(source, target, own_sem.at[len(started)]))
+                    own_mid[sem][-1].start()
+                    started.append(sem)
+
+    def over_base(part, k):
+        rows = pl.ds(8 * part, 8) if part < 2 else pl.ds(0, 16)
+        sem = 4 * part + k if part < 2 else 8
+        offsets = (0,) if part == 2 else range(4) if k < 3 else FAR
         to_y = (my_y + TURNS[k]) % 4
-        rows = pl.ds(8 * part, 8)
-        sem = 4 * part + k + int(bool(own_chip))
         for own in own_mid[sem]:
             own.wait()
-        count = {None: 4, False: 3, True: 1}[own_chip]
-        wait_for(out_ref.at[pl.ds(0, count), 0, :, pl.ds(0, N_BAND - 1), rows, :], mid_sem.at[sem])
-        for x in {None: range(4), False: (2, 1, 3), True: (0,)}[own_chip]:
+        wait_for(out_ref.at[pl.ds(0, len(offsets)), 0, :, pl.ds(0, N_BAND - 1), rows, :], mid_sem.at[sem])
+        for x in offsets:
             for core in range(2):
                 held = mid_ref.at[(my_x + x) % 4, to_y, (my_core + core) % 2, :, rows, :]
                 target = in_ref.at[base, :, rows, :]
                 if (x, TURNS[k], core) == (0, 0, 0):
-                    own = pltpu.make_async_copy(held, target, own_sem.at[11 + part])
+                    own = pltpu.make_async_copy(held, target, own_sem.at[13])
                     own.start()
                     own_in.append(own)
                 else:
@@ -443,11 +449,10 @@
 
     def first(k):
         for part in range(2):
-            for i, count in enumerate(((8,), (7,), (6, 1))[0 if TURNS[k] else 1 + part]):
-                came = in_ref.at[pl.ds(0, count), :, pl.ds(8 * part, 8), :]
-                wait_for(came, recv_sem.at[4 * part + k + i])
-            if TURNS[k] == 0:
-                own_in[part].wait()
+            wait_for(in_ref.at[pl.ds(0, 8 if k < 3 else 6), :, pl.ds(8 * part, 8), :], recv_sem.at[4 * part + k])
+        if k == 3:
+            wait_for(in_ref.at[0], recv_sem.at[8])
+            own_in[0].wait()
         from_y = (my_y - TURNS[k] + 4) % 4
 
         ids = [t // 2 * 8 + from_y * 2 + t % 2 for t in range(8)]
@@ -484,9 +489,9 @@
     first(0)
     over_base(1, 2)
     first(1)
-    over_base(1, 3, False)
+    over_base(1, 3)
     first(2)
-    over_base(1, 3, True)
+    over_base(2, 3)
     first(3)
     wait_for(in_ref.at[pl.ds(0, 28)], send_sem)
     wait_for(in_ref.at[pl.ds(0, 31)], send_sem)
@@ -590,7 +595,7 @@
             dma,
             dma((9,)),
             dma((9,)),
-            dma((13,)),
+            dma((14,)),
         ],
         compiler_params=pltpu.CompilerParams(vmem_limit_bytes=56 * 2**20, collective_id=1, has_side_effects=True),
         name="exchange",

time: 114 us -> 113 us (level)
  no operation moved by 1% of the time
where the time goes in v7:
time: 113 us; the launch traced here: 112 us
  Pallas kernels  112 us (99%)
    pallas_call x1, Pallas kernels, shards(): pl.pallas_call(exchange_kernel, out_shape=jax.ShapeDtypeStruct((2, TILE *...  62.9 us
    pallas_call x1, Pallas kernels, shards(): pl.pallas_call(grid_kernel, out_shape=(jax.ShapeDtypeStruct((N_BASE, PAIR...  33.6 us
    pallas_call x1, Pallas kernels, shards(): pl.pallas_call(row_kernel, out_shape=jax.ShapeDtypeStruct((G // 2, 128),...  11.3 us
    pallas_call x1, Pallas kernels, shards(): pl.pallas_call(column_kernel, out_shape=jax.ShapeDtypeStruct((2, TILE, G)...  4.62 us

profile of v7, /device:TPU:1, one launch (start us, length us, event | category | flops | bytes accessed | tf_op | source)
XLA Modules:
  0.0 112.5 jit_solution(8809900810212812292)
XLA Ops:
  0.0 33.6 %gridding.1 = (f32[32,128,128]{2,1,0:T(8,128)}, s32[32,2,128]{2,1,0:T(2,128)}) custom-call(f32[256,2,128]{2,1,0:T(2,128)} %vis_ref.1, f32[2,8,256]{2,1,0:T(8,128)} %bitcast.4, f32[1,16]{1,0:T(1,128)} %bitcast.7, s32[2,128]{1,0:T(2,128)} %bitcast.5, s32[2,128]{1,0:T(2,128)} %bitcast.6, f32[32,32]{1,0:T(8,128)} %taper_in_ref.1, ...), custom_call_target="tpu_custom_call" | custom-call | tf_op jit(solution)/shard_map/gridding/pallas_call | solution.py:533
  33.6 11.3 %rows.1.rows_ref = f32[4096,128]{1,0:T(8,128)} custom-call(f32[32,128,128]{2,1,0:T(8,128)} %get-tuple-element.7.all_ref, s32[32,2,128]{2,1,0:T(2,128)} %get-tuple-element.8.all_ids_ref), custom_call_target="tpu_custom_call" | custom-call | tf_op jit(solution)/shard_map/rows/pallas_call | solution.py:564
  45.0 62.9 %exchange.1.v_ref = f32[2,2304,128]{2,1,0:T(8,128)} custom-call(f32[4096,128]{1,0:T(8,128)} %rows.1.rows_ref, bf16[256,512]{1,0:T(8,128)(2,1)} %constant.47.clone.reh_ref, bf16[256,512]{1,0:T(8,128)(2,1)} %constant.48.clone.rel_ref, f32[32,256]{1,0:T(8,128)} %constant.43.clone.rtc_ref.tc_ref, f32[32,256]{1,0:T(8,128)} %constant.44.clone.rts_ref.ts_ref, ...), custom_call_target="tpu_custom_call" | custom-call | tf_op jit(solution)/shard_map/exchange/pallas_call | solution.py:583
  107.8 4.6 %columns.1 = f32[2,32,8192]{2,1,0:T(8,128)} custom-call(f32[2,2304,128]{2,1,0:T(8,128)} %exchange.1.v_ref, bf16[64,64]{1,0:T(8,128)(2,1)} %constant.45.clone.fh_ref, bf16[64,64]{1,0:T(8,128)(2,1)} %constant.46.clone.fl_ref), custom_call_target="tpu_custom_call" | custom-call | tf_op jit(solution)/shard_map/columns/pallas_call | solution.py:603

commit v8 on v7

--- a/solution.py
+++ b/solution.py
@@ -347,8 +347,8 @@
 
 
 def exchange_kernel(
-    rows_ref, reh_ref, rel_ref, rtc_ref, rts_ref, rfh_ref, rfl_ref, eh_ref, el_ref, tc_ref, ts_ref,
-    v_ref, held_ref, z_ref, out_ref, mid_ref, in_ref, load_sem, send_sem, mid_sem, recv_sem, own_sem,
+    rows_ref, reh_ref, rel_ref, rtc_ref, rts_ref, rfh_ref, rfl_ref, eh_in, el_in, tc_ref, ts_ref,
+    v_ref, eh_ref, el_ref, held_ref, z_ref, out_ref, mid_ref, in_ref, load_sem, send_sem, mid_sem, recv_sem, own_sem,
 ):
     base, band = lax.axis_index("base"), lax.axis_index("band")
     my_x, my_y, my_core = base // 8, base // 2 % 4, base % 2
@@ -357,6 +357,9 @@
         part = pl.ds(i * 4 * K_TILES, 4 * K_TILES)
         loads.append(pltpu.make_async_copy(rows_ref.at[part, :], held_ref.at[part, :], load_sem.at[i]))
         loads[i].start()
+    for source, target in ((eh_in, eh_ref), (el_in, el_ref)):
+        loads.append(pltpu.make_async_copy(source, target, load_sem.at[len(loads)]))
+        loads[-1].start()
     barrier = pltpu.get_barrier_semaphore()
     for step in range(1, N_BAND):
         pl.semaphore_signal(barrier, inc=1, device_id=(base, (band + step) % N_BAND), device_id_type=MESH)
@@ -448,14 +451,17 @@
                     send_to(held, target, send_sem, recv_sem.at[sem], to)
 
     def first(k):
-        for part in range(2):
-            wait_for(in_ref.at[pl.ds(0, 8 if k < 3 else 6), :, pl.ds(8 * part, 8), :], recv_sem.at[4 * part + k])
-        if k == 3:
+        if k < 4:
+            for part in range(2):
+                came = in_ref.at[pl.ds(0, 8 if k < 3 else 6), :, pl.ds(8 * part, 8), :]
+                wait_for(came, recv_sem.at[4 * part + k])
+        else:
             wait_for(in_ref.at[0], recv_sem.at[8])
             own_in[0].wait()
-        from_y = (my_y - TURNS[k] + 4) % 4
-
-        ids = [t // 2 * 8 + from_y * 2 + t % 2 for t in range(8)]
+        from_y = (my_y - TURNS[min(k, 3)] + 4) % 4
+
+        columns = range(4) if k < 3 else [(my_x + x) % 4 for x in (FAR if k == 3 else (0,))]
+        ids = [x * 8 + from_y * 2 + core for x in columns for core in range(2)]
         lefts = []
         for j in ids:
             turned = in_ref[j].reshape(128, 128).T
@@ -484,6 +490,8 @@
             over_band(part, k)
     for k in range(4):
         over_base(0, k)
+    for load in loads[4:]:
+        load.wait()
     over_base(1, 0)
     over_base(1, 1)
     first(0)
@@ -493,6 +501,7 @@
     first(2)
     over_base(2, 3)
     first(3)
+    first(4)
     wait_for(in_ref.at[pl.ds(0, 28)], send_sem)
     wait_for(in_ref.at[pl.ds(0, 31)], send_sem)
 
@@ -583,15 +592,17 @@
     turned = pl.pallas_call(
         exchange_kernel,
         out_shape=jax.ShapeDtypeStruct((2, TILE * PITCH, 128), F32),
-        in_specs=[HBM] + [VMEM] * 10,
+        in_specs=[HBM] + [VMEM] * 6 + [HBM] * 2 + [VMEM] * 2,
         out_specs=VMEM,
         scratch_shapes=[
+            pltpu.VMEM(tables[0].shape, BF16),
+            pltpu.VMEM(tables[1].shape, BF16),
             pltpu.VMEM((G // 2, 128), F32),
             pltpu.VMEM((2, 16 * Z_PITCH, 128), F32),
             by_target,
             by_target,
             pltpu.VMEM((N_BASE, N_BAND, 16, 128), F32),
-            dma((4,)),
+            dma((6,)),
             dma,
             dma((9,)),
             dma((9,)),

time: 113 us -> 113 us (level)
  no operation moved by 1% of the time
where the time goes in v8:
time: 113 us
  Pallas kernels  113 us (100%)
    pallas_call x1, Pallas kernels, shards(): pl.pallas_call(exchange_kernel, out_shape=jax.ShapeDtypeStruct((2, TILE *...  62.9 us
    pallas_call x1, Pallas kernels, shards(): pl.pallas_call(grid_kernel, out_shape=(jax.ShapeDtypeStruct((N_BASE, PAIR...  33.6 us
    pallas_call x1, Pallas kernels, shards(): pl.pallas_call(row_kernel, out_shape=jax.ShapeDtypeStruct((G // 2, 128),...  11.3 us
    pallas_call x1, Pallas kernels, shards(): pl.pallas_call(column_kernel, out_shape=jax.ShapeDtypeStruct((2, TILE, G)...  4.62 us

profile of v8, /device:TPU:1, one launch (start us, length us, event | category | flops | bytes accessed | tf_op | source)
XLA Modules:
  0.0 112.5 jit_solution(7780921796629763848)
XLA Ops:
  0.0 33.6 %gridding.1 = (f32[32,128,128]{2,1,0:T(8,128)}, s32[32,2,128]{2,1,0:T(2,128)}) custom-call(f32[256,2,128]{2,1,0:T(2,128)} %vis_ref.1, f32[2,8,256]{2,1,0:T(8,128)} %bitcast.4, f32[1,16]{1,0:T(1,128)} %bitcast.7, s32[2,128]{1,0:T(2,128)} %bitcast.5, s32[2,128]{1,0:T(2,128)} %bitcast.6, f32[32,32]{1,0:T(8,128)} %taper_in_ref.1, ...), custom_call_target="tpu_custom_call" | custom-call | tf_op jit(solution)/shard_map/gridding/pallas_call | solution.py:542
  33.6 11.3 %rows.1.rows_ref = f32[4096,128]{1,0:T(8,128)} custom-call(f32[32,128,128]{2,1,0:T(8,128)} %get-tuple-element.7.all_ref, s32[32,2,128]{2,1,0:T(2,128)} %get-tuple-element.8.all_ids_ref), custom_call_target="tpu_custom_call" | custom-call | tf_op jit(solution)/shard_map/rows/pallas_call | solution.py:573
  45.0 62.9 %exchange.1.v_ref = f32[2,2304,128]{2,1,0:T(8,128)} custom-call(f32[4096,128]{1,0:T(8,128)} %rows.1.rows_ref, bf16[256,512]{1,0:T(8,128)(2,1)} %constant.47.clone.reh_ref, bf16[256,512]{1,0:T(8,128)(2,1)} %constant.48.clone.rel_ref, f32[32,256]{1,0:T(8,128)} %constant.43.clone.rtc_ref.tc_ref, f32[32,256]{1,0:T(8,128)} %constant.44.clone.rts_ref.ts_ref, ...), custom_call_target="tpu_custom_call" | custom-call | tf_op jit(solution)/shard_map/exchange/pallas_call | solution.py:592
  107.9 4.6 %columns.1 = f32[2,32,8192]{2,1,0:T(8,128)} custom-call(f32[2,2304,128]{2,1,0:T(8,128)} %exchange.1.v_ref, bf16[64,64]{1,0:T(8,128)(2,1)} %constant.45.clone.fh_ref, bf16[64,64]{1,0:T(8,128)(2,1)} %constant.46.clone.fl_ref), custom_call_target="tpu_custom_call" | custom-call | tf_op jit(solution)/shard_map/columns/pallas_call | solution.py:614
